TPU v7x, 512 devices: a whole 4x4x16 slice. The times are simulated.
512 devices in a mesh: rep: 4 (over y), samp: 4 (over z_hi), tp: 32 (over z_lo, x, core).
Axes of the slice: x: 4, y: 4, z: 16 (z_hi: 4, z_lo: 4; z = z_hi * 4 + z_lo), core: 2. Of those that a mesh axis runs over, the one named last changes fastest.
Arguments:
- prompt_tokens: bfloat16 [256, 4, 8192], P(None, 'rep', 'samp'), may hold values from -6 to 6
- step_tokens: bfloat16 [4, 16, 4, 8192], P(None, None, 'rep', 'samp'), may hold values from -6 to 6
- lengths: int32 [16, 4], P('samp', 'rep'), may hold values from 1 to 4, as said below
- input_weight: bfloat16 [2, 8192, 8192], P(None, 'samp', 'tp'), may hold values from -0.0625 to 0.0625
- group_weight: bfloat16 [8192, 2048], P('samp', 'tp'), may hold values from -0.0625 to 0.0625
- step_weight: bfloat16 [8192, 128], P('samp', 'tp'), may hold values from -0.0625 to 0.0625
- conv_weight: float32 [4, 8192], P(None, 'tp'), may hold values from -3 to 3
- group_conv: float32 [4, 2048], P(None, 'tp'), may hold values from -3 to 3
- conv_bias: float32 [8192], P('tp'), may hold values from -3 to 3
- group_bias: float32 [2048], P('tp'), may hold values from -3 to 3
- step_bias: float32 [128], P('tp'), may hold values from -3 to -1
- decay_log: float32 [128], P('tp'), may hold values from -4.6 to -1.6
- skip_gain: float32 [128], P('tp'), may hold values from 0.5 to 1.5
- norm_gain: float32 [8192], P('tp'), may hold values from 0.5 to 1.5
- output_weight: bfloat16 [8192, 8192], P('tp', 'samp'), may hold values from -0.125 to 0.125
Outputs:
- prefill_out: bfloat16 [256, 4, 8192], P('samp', 'rep', 'tp')
- decode_out: bfloat16 [4, 16, 4, 8192], P(None, 'samp', 'rep', 'tp')
Inputs may be any that keep to these rules, and one draw needn't show every extreme that they name: `lengths`: every prompt has a sample that decodes all 4 steps.
All inputs are finite; a program needn't handle non-finite values.
Results may differ from a plain program's by a relative error of at most 0.035.
Values may be sent and summed in bfloat16 or wider, within the bound.
A program may use at most 64 MiB of HBM per device.

v0:
```python
import jax
import jax.numpy as jnp
from jax import lax
from jax.sharding import PartitionSpec as P

HEADS = 128
HEAD_DIM = 64
STATE = 128
GROUPS = 8
CONV = 4


HIGHEST_PRECISION = lax.Precision.HIGHEST


def shifted(block, axis, distance):
    devices = range(lax.axis_size(axis))
    route = [(i - distance, i) for i in devices if i - distance in devices]
    return lax.ppermute(block, axis, route)


def carried_in(x, axis, join, neutral):
    place = lax.axis_index(axis)
    gathered = jax.tree.map(
        lambda a, kind: lax.all_gather(a.astype(kind), axis), x, (jnp.bfloat16, jnp.bfloat16)
    )
    state = jax.tree.map(lambda a, e: jnp.zeros_like(a) + jnp.asarray(e, a.dtype), x, neutral)

    def one(turn, state):
        return join(
            state,
            jax.tree.map(
                lambda a, own: lax.dynamic_index_in_dim(a, turn, 0, False).astype(own.dtype),
                gathered,
                x,
            ),
        )

    return lax.fori_loop(0, place, one, state)


def shortened(x):
    return jax.tree.map(lambda a: a.astype(jnp.bfloat16) if a.dtype == jnp.float32 else a, x)


def spread(value, axis, source):
    kept = jnp.where(lax.axis_index(axis) == source, value, 0).astype(value.dtype)
    return lax.psum(kept, axis)


def convolve(window, tap_weight, tap_bias):
    length = window.shape[0] - CONV + 1
    running = jnp.zeros(window[:length].shape, jnp.float32) + tap_bias
    for tap_index in range(CONV):
        running = running + tap_weight[tap_index] * window[tap_index : tap_index + length].astype(
            jnp.float32
        )
    return jax.nn.silu(running).astype(jnp.bfloat16)


def head_inputs(mixed, heads_here):
    inner_here = heads_here * HEAD_DIM
    leading = mixed.shape[:-1]
    head_values = (
        mixed[..., :inner_here].astype(jnp.float32).reshape(leading + (heads_here, HEAD_DIM))
    )
    everyone = lax.all_gather(mixed[..., inner_here:], "tp", axis=2, tiled=True)
    per_group = HEADS // GROUPS
    own_count = max(1, heads_here // per_group)
    first_group = lax.axis_index("tp") * heads_here // per_group
    grouped = everyone.reshape(leading + (2, STATE, GROUPS))
    own_groups = lax.dynamic_slice_in_dim(grouped, first_group, own_count, len(leading) + 2).astype(
        jnp.float32
    )
    own_groups = jnp.swapaxes(own_groups, -1, -2)
    repeats = heads_here // own_count
    input_map = jnp.repeat(own_groups[..., 0, :, :], repeats, axis=len(leading))
    output_map = jnp.repeat(own_groups[..., 1, :, :], repeats, axis=len(leading))
    return (head_values, input_map, output_map)


def block_scan(head_values, input_map, output_map, step_size, log_decay):
    row_total = head_values.shape[0]
    block_rows = min(row_total, 128)
    block_count = row_total // block_rows
    causal = jnp.arange(block_rows)[:, None] >= jnp.arange(block_rows)[None, :]

    def as_blocks(array):
        return array.reshape((block_count, block_rows) + array.shape[1:])

    def one_block(state, pieces):
        values, inputs, readout, step_sizes, log_steps = pieces
        running = jnp.cumsum(log_steps, axis=0)
        trail = jnp.moveaxis(running, 0, -1)
        gaps = trail[..., :, None] - trail[..., None, :]
        size_trail = jnp.moveaxis(step_sizes, 0, -1)
        weight = jnp.where(causal, jnp.exp(jnp.minimum(gaps, 0.0)), 0.0) * size_trail[..., None, :]
        intersections = jnp.einsum(
            "ibhn,jbhn->bhij",
            readout.astype(jnp.bfloat16),
            inputs.astype(jnp.bfloat16),
            preferred_element_type=jnp.float32,
        )
        scores = intersections * weight
        within = jnp.einsum("bhij,jbhp->ibhp", scores, values, precision=HIGHEST_PRECISION)
        carried = (
            jnp.einsum("ibhn,bhpn->ibhp", readout, state, precision=HIGHEST_PRECISION)
            * jnp.exp(running)[..., None]
        )
        block_total = running[-1]
        tail_weight = jnp.exp(block_total[None] - running) * step_sizes
        update = jnp.einsum(
            "jbhp,jbhn->bhpn", values * tail_weight[..., None], inputs, precision=HIGHEST_PRECISION
        )
        return (jnp.exp(block_total)[..., None, None] * state + update, within + carried)

    zero_state = jnp.zeros(head_values.shape[1:3] + (HEAD_DIM, STATE), jnp.float32)
    pieces = (
        as_blocks(head_values),
        as_blocks(input_map),
        as_blocks(output_map),
        as_blocks(step_size),
        as_blocks(log_decay),
    )
    final_state, outputs = lax.scan(one_block, zero_state, pieces)
    return (
        outputs.reshape((row_total,) + outputs.shape[2:]),
        final_state,
        jnp.sum(log_decay, axis=0),
    )


def chain_states(earlier, later):
    return (earlier[0] * later[0], later[0][..., None, None] * earlier[1] + later[1])


def project_out(reading, gate_rows, norm_gain, full_output):
    leading = reading.shape[:-2]
    heads_here = reading.shape[-2]
    gated = reading.reshape(leading + (heads_here * HEAD_DIM,)) * jax.nn.silu(
        gate_rows.astype(jnp.float32)
    )
    per_group = HEADS // GROUPS
    own_count = max(1, heads_here // per_group)
    first_group = lax.axis_index("tp") * heads_here // per_group
    split_gated = gated.reshape(leading + (own_count, gated.shape[-1] // own_count))
    squares = jnp.sum(split_gated * split_gated, axis=-1)
    placed = lax.dynamic_update_slice_in_dim(
        jnp.zeros(leading + (GROUPS,), jnp.float32), squares, first_group, 2
    )
    totals = lax.psum(placed, "tp")
    own_totals = lax.dynamic_slice_in_dim(totals, first_group, own_count, 2)
    scale = lax.rsqrt(own_totals / (HEADS * HEAD_DIM // GROUPS) + 1e-05)
    normed = ((split_gated * scale[..., None]).reshape(gated.shape) * norm_gain).astype(
        jnp.bfloat16
    )
    partial_sums = jnp.einsum(
        "sbi,id->sbd", normed, full_output, preferred_element_type=jnp.float32
    )
    return lax.psum_scatter(
        partial_sums.astype(jnp.bfloat16), "tp", scatter_dimension=2, tiled=True
    )


def shards(
    prompt_tokens,
    step_tokens,
    lengths,
    input_weight,
    group_weight,
    step_weight,
    conv_weight,
    group_conv,
    conv_bias,
    group_bias,
    step_bias,
    decay_log,
    skip_gain,
    norm_gain,
    output_weight,
):
    heads_here = decay_log.shape[0]
    inner_here = heads_here * HEAD_DIM
    group_here = group_weight.shape[1]
    samp_count = lax.axis_size("samp")
    rim_rows = CONV - 1
    weights = jnp.concatenate([input_weight[0], input_weight[1], group_weight, step_weight], axis=1)
    tap_weight = jnp.concatenate([conv_weight, group_conv], axis=1)
    tap_bias = jnp.concatenate([conv_bias, group_bias])
    rate = jnp.exp(decay_log)
    full_output = lax.all_gather(output_weight, "samp", axis=1, tiled=True)
    projected = lax.psum_scatter(
        jnp.einsum(
            "lbd,dc->lbc", prompt_tokens, weights, preferred_element_type=jnp.float32
        ).astype(jnp.bfloat16),
        "samp",
        scatter_dimension=0,
        tiled=True,
    )
    mixed_pre = projected[..., inner_here : 2 * inner_here + group_here]
    earlier = shifted(mixed_pre[-rim_rows:], "samp", 1)
    mixed = convolve(jnp.concatenate([earlier, mixed_pre], axis=0), tap_weight, tap_bias)
    head_values, input_map, output_map = head_inputs(mixed, heads_here)
    step_size = jax.nn.softplus(projected[..., -heads_here:].astype(jnp.float32) + step_bias)
    log_decay = -step_size * rate
    outputs, final_state, log_total = block_scan(
        head_values, input_map, output_map, step_size, log_decay
    )
    outputs = outputs + skip_gain[:, None] * head_values
    carried = carried_in(
        (jnp.exp(log_total), final_state),
        "samp",
        chain_states,
        (jnp.ones_like(log_total), jnp.zeros_like(final_state)),
    )
    incoming = carried[1]
    outputs = (
        outputs
        + jnp.einsum("ibhn,bhpn->ibhp", output_map, incoming, precision=HIGHEST_PRECISION)
        * jnp.exp(jnp.cumsum(log_decay, axis=0))[..., None]
    )
    final_state = jnp.exp(log_total)[..., None, None] * incoming + final_state
    forked, window = (
        spread(shortened(final_state), "samp", samp_count - 1).astype(final_state.dtype),
        spread(
            mixed_pre[-rim_rows:].astype(jnp.float32).astype(jnp.bfloat16), "samp", samp_count - 1
        ).astype(jnp.float32),
    )
    window = window.astype(jnp.bfloat16)
    gate_rows = projected[..., :inner_here]
    prefill_out = project_out(outputs, gate_rows, norm_gain, full_output)
    samples_here = lengths.shape[0]
    state = jnp.broadcast_to(forked[None], (samples_here,) + forked.shape)
    window = jnp.broadcast_to(window[:, None], (rim_rows, samples_here) + window.shape[1:])
    every_step = lax.psum_scatter(
        jnp.einsum(
            "tsbd,dc->tsbc", step_tokens, weights, preferred_element_type=jnp.float32
        ).astype(jnp.bfloat16),
        "samp",
        scatter_dimension=1,
        tiled=True,
    )
    results = []
    for step_index in range(step_tokens.shape[0]):
        fresh = every_step[step_index]
        full_window = jnp.concatenate(
            [window, fresh[..., inner_here : 2 * inner_here + group_here][None]], axis=0
        )
        mixed_now = convolve(full_window, tap_weight, tap_bias)[0]
        values_now, inputs_now, readout_now = head_inputs(mixed_now, heads_here)
        size_now = jax.nn.softplus(fresh[..., -heads_here:].astype(jnp.float32) + step_bias)
        decay_now = jnp.exp(-size_now * rate)
        advanced = (
            decay_now[..., None, None] * state
            + (size_now[..., None] * values_now)[..., None] * inputs_now[..., None, :]
        )
        reading = (
            jnp.sum(advanced * readout_now[..., None, :], axis=-1) + skip_gain[:, None] * values_now
        )
        active = step_index < lengths
        state = jnp.where(active[..., None, None, None], advanced, state)
        window = jnp.where(active[None, ..., None], full_window[1:], window)
        produced = project_out(reading, fresh[..., :inner_here], norm_gain, full_output)
        results.append(jnp.where(active[..., None], produced, jnp.zeros_like(produced)))
    return (prefill_out, jnp.stack(results))


def solution(mesh):
    placed = (
        P(None, "rep", "samp"),
        P(None, None, "rep", "samp"),
        P("samp", "rep"),
        P(None, "samp", "tp"),
        P("samp", "tp"),
        P("samp", "tp"),
        P(None, "tp"),
        P(None, "tp"),
        P("tp"),
        P("tp"),
        P("tp"),
        P("tp"),
        P("tp"),
        P("tp"),
        P("tp", "samp"),
    )
    return jax.shard_map(
        shards,
        mesh=mesh,
        in_specs=placed,
        out_specs=(P("samp", "rep", "tp"), P(None, "samp", "rep", "tp")),
        check_vma=False,
    )
```

profile of v0, /device:TPU:24, one launch (start us, length us, event | category | flops | bytes accessed | tf_op | source)
XLA Modules:
  0.0 1400.2 jit_solution(10627004256836115280)
XLA Ops:
  7.2 1.8 fusion.111
  9.0 1.4 copy.154
  10.4 0.6 copy.155
  11.2 2.2 fusion.7
  13.4 0.9 copy.148
  15.8 2.5 fusion.16
  18.3 38.9 %reduce-scatter.20.cloned.1.call-done = bf16[64,580]{1,0:T(8,128)(2,1)} async-done(((bf16[256,580]{1,0:T(8,128)(2,1)}), bf16[64,580]{1,0:T(8,128)(2,1)}) %reduce-scatter.20.cloned.1.call-update) | async-done | bytes 74256
  57.2 1.0 copy.149
  59.1 28.0 %all-reduce.3 = (bf16[16]{0:T(256)(128)(2,1)S(1)}, bf16[3,1,320]{0,2,1:T(8,128)(2,1)S(1)}) all-reduce(bf16[16]{0:T(256)(128)(2,1)S(1)} %dynamic-update-slice, bf16[3,1,320]{0,2,1:T(8,128)(2,1)S(1)} %get-tuple-element.148), channel_id=2, replica_groups=mesh['rep'=4,'samp'=4,'tp'=32] {'samp'}, use_global_device_ids=true, to_apply=%add | all-reduce | flops 976 | bytes 3904
  87.3 1.7 collective-permute-start
  89.2 1.8 collective-permute-done
  91.5 45.3 %all_gather.28 = bf16[64,1,2048]{0,2,1:T(8,128)(2,1)S(1)} all-gather(bf16[64,1,64]{0,2,1:T(8,128)(2,1)S(1)} %slice.296), channel_id=1, replica_groups=mesh['rep'=4,'samp'=4,'tp'=32] {'tp'}, dimensions={2}, use_global_device_ids=true | all-gather | bytes 270336 | tf_op jit(solution)/shard_map/all_gather | solution.py:67
  137.3 21.1 %all-gather.1 = bf16[16,64,128]{2,1,0:T(8,128)(2,1)S(1)} all-gather(bf16[4,64,128]{2,1,0:T(8,128)(2,1)S(1)} %get-tuple-element.197), channel_id=3, replica_groups=mesh['rep'=4,'samp'=4,'tp'=32] {'samp'}, dimensions={0}, use_global_device_ids=true | all-gather | bytes 327680 | tf_op jit(solution)/shard_map/all_gather | solution.py:25
  158.4 0.7 fusion.33
  159.2 0.7 all-gather.4.cloned.1.call-update
  162.9 60.0 %all-reduce.7.cloned.1.call-done = (bf16[4,16,1,580]{3,1,0,2:T(8,128)(2,1)}, bf16[4,64,128]{2,1,0:T(8,128)(2,1)}) async-done(((bf16[4,16,1,580]{3,1,0,2:T(8,128)(2,1)}, bf16[4,64,128]{2,1,0:T(8,128)(2,1)}), (bf16[4,16,1,580]{3,1,0,2:T(8,128)(2,1)}, bf16[4,64,128]{2,1,0:T(8,128)(2,1)})) %all-reduce.7.cloned.1.call-update) | async-done | bytes 139792
  222.9 0.8 dynamic-slice_bitcast_fusion
  223.8 0.7 dynamic-slice_bitcast_fusion.1
  225.6 0.8 broadcast_in_dim.198
  226.5 101.3 %all_gather.33 = bf16[4,1,2048]{0,1,2:T(2,128)(2,1)S(1)} all-gather(bf16[4,1,64]{0,1,2:T(2,128)(2,1)S(1)} %copy.125), channel_id=1, replica_groups=mesh['rep'=4,'samp'=4,'tp'=32] {'tp'}, dimensions={2}, use_global_device_ids=true | all-gather | bytes 16896 | tf_op jit(solution)/shard_map/all_gather | solution.py:67
  328.7 79.3 %all_gather.36 = bf16[4,1,2048]{0,1,2:T(2,128)(2,1)S(1)} all-gather(bf16[4,1,64]{0,1,2:T(2,128)(2,1)S(1)} %copy.134), channel_id=1, replica_groups=mesh['rep'=4,'samp'=4,'tp'=32] {'tp'}, dimensions={2}, use_global_device_ids=true | all-gather | bytes 16896 | tf_op jit(solution)/shard_map/all_gather | solution.py:67
  409.0 43.2 %all_gather.35 = bf16[4,1,2048]{0,1,2:T(2,128)(2,1)S(1)} all-gather(bf16[4,1,64]{0,1,2:T(2,128)(2,1)S(1)} %copy.132), channel_id=1, replica_groups=mesh['rep'=4,'samp'=4,'tp'=32] {'tp'}, dimensions={2}, use_global_device_ids=true | all-gather | bytes 16896 | tf_op jit(solution)/shard_map/all_gather | solution.py:67
  453.1 40.7 %all_gather.34 = bf16[4,1,2048]{0,1,2:T(2,128)(2,1)S(1)} all-gather(bf16[4,1,64]{0,1,2:T(2,128)(2,1)S(1)} %copy.129), channel_id=1, replica_groups=mesh['rep'=4,'samp'=4,'tp'=32] {'tp'}, dimensions={2}, use_global_device_ids=true | all-gather | bytes 16896 | tf_op jit(solution)/shard_map/all_gather | solution.py:67
  496.5 1.3 multiply_reduce_fusion.1
  498.4 135.0 %all-reduce.2 = (f32[64,1,8]{0,2,1:T(8,128)S(1)}, f32[4,1,8]{0,2,1:T(8,128)S(1)}, f32[4,1,8]{0,2,1:T(8,128)S(1)}, f32[4,1,8]{0,2,1:T(8,128)S(1)}, f32[4,1,8]{0,2,1:T(8,128)S(1)}) all-reduce(f32[64,1,8]{0,2,1:T(8,128)S(1)} %dynamic_update_slice.18, ...), channel_id=1, replica_groups=mesh['rep'=4,'samp'=4,'tp'=32] {'tp'}, use_global_device_ids=true, to_apply=%region_7.8 | all-reduce | flops 640 | bytes 5120 | tf_op jit(solution)/shard_map/psum | solution.py:151
  633.5 2.9 fusion.4
  636.4 6.8 copy.146
  643.2 3.9 copy.160
  647.1 2.9 fusion.3
  650.0 6.8 copy.144
  656.8 3.8 copy.161
  660.6 2.9 fusion.2
  663.5 6.8 copy.142
  670.3 3.8 copy.162
  674.2 2.9 fusion.1
  677.1 6.8 copy.140
  683.9 3.8 copy.163
  687.8 4.2 fusion
  691.9 98.5 %reduce-scatter.28.cloned.1.call-done = bf16[256,4]{1,0:T(8,128)(2,1)} async-done(((bf16[8192,4]{1,0:T(8,128)(2,1)}), bf16[256,4]{1,0:T(8,128)(2,1)}) %reduce-scatter.28.cloned.1.call-update) | async-done | bytes 2064
  790.4 0.9 reshape_bitcast_fusion
  791.4 149.9 %reduce-scatter.26.cloned.1.call-done = bf16[256,4]{1,0:T(8,128)(2,1)} async-done(((bf16[8192,4]{1,0:T(8,128)(2,1)}), bf16[256,4]{1,0:T(8,128)(2,1)}) %reduce-scatter.26.cloned.1.call-update) | async-done | bytes 2064
  941.3 0.9 reshape_bitcast_fusion.1
  942.3 150.1 %reduce-scatter.24.cloned.1.call-done = bf16[256,4]{1,0:T(8,128)(2,1)} async-done(((bf16[8192,4]{1,0:T(8,128)(2,1)}), bf16[256,4]{1,0:T(8,128)(2,1)}) %reduce-scatter.24.cloned.1.call-update) | async-done | bytes 2064
  1092.4 0.9 reshape_bitcast_fusion.2
  1093.4 150.0 %reduce-scatter.22.cloned.1.call-done = bf16[256,4]{1,0:T(8,128)(2,1)} async-done(((bf16[8192,4]{1,0:T(8,128)(2,1)}), bf16[256,4]{1,0:T(8,128)(2,1)}) %reduce-scatter.22.cloned.1.call-update) | async-done | bytes 2064
  1243.4 0.9 reshape_bitcast_fusion.3
  1244.7 0.6 pad_maximum_fusion.7
  1245.4 148.0 %reduce-scatter.18.cloned.1.call-done = bf16[64,1,256]{2,0,1:T(8,128)(2,1)} async-done(((bf16[64,1,8192]{2,0,1:T(8,128)(2,1)}), bf16[64,1,256]{2,0,1:T(8,128)(2,1)}) %reduce-scatter.18.cloned.1.call-update) | async-done | bytes 32784 | tf_op jit(solution)/shard_map/reduce_scatter | solution.py:160
  (167 shorter events, 13.5 us)
Async XLA Ops:
  7.2 3.9 copy-start
  7.2 3.9 copy-start.10
  7.2 50.0 %reduce-scatter.20.cloned.1.call-start = ((), (), s32[]{:S(2)}) async-start(), calls=%async_computation.8 | async-start | bytes 409600
  11.1 3.3 copy-start.7
  11.1 3.3 copy-start.11
  11.1 3.4 copy-start.12
  11.1 3.4 copy-start.8
  11.1 4.6 copy-start.4
  11.2 4.6 copy-start.6
  11.2 4.6 copy-start.1
  14.3 208.5 %all-reduce.7.cloned.1.call-start = ((), (), s32[]{:S(2)}) async-start(), calls=%async_computation.13 | async-start | bytes 294912
  15.8 42.4 %copy-start.3 = (f32[4]{0:T(128)S(1)}, f32[4]{0:T(128)}, u32[]{:S(2)}) copy-start(f32[4]{0:T(128)} %param.27) | copy-start | bytes 52
  18.3 141.6 %copy-start.5 = (f32[4]{0:T(128)S(1)}, f32[4]{0:T(128)}, u32[]{:S(2)}) copy-start(f32[4]{0:T(128)} %param.29) | copy-start | bytes 52
  18.3 141.7 %copy-start.9 = (s32[4,1]{0,1:T(1,128)S(1)}, s32[4,1]{0,1:T(1,128)}, u32[]{:S(2)}) copy-start(s32[4,1]{0,1:T(1,128)} %param.19) | copy-start | bytes 52
  87.3 3.7 collective-permute-start
  159.1 474.4 %all-gather.4.cloned.1.call-start = ((), (), s32[]{:S(2)}) async-start(), calls=%async_computation.6 | async-start | bytes 5242880 | tf_op jit(solution)/shard_map/all_gather | solution.py:191
  159.8 630.6 %reduce-scatter.28.cloned.1.call-start = ((), (), s32[]{:S(2)}) async-start(), calls=%async_computation.12 | async-start | bytes 2162688
  408.0 225.5 %copy-start.2 = (f32[256]{0:T(256)S(1)}, f32[256]{0:T(256)}, u32[]{:S(2)}) copy-start(f32[256]{0:T(256)} %param.30) | copy-start | bytes 3076
  647.1 294.2 %reduce-scatter.26.cloned.1.call-start = ((), (), s32[]{:S(2)}) async-start(), calls=%async_computation.11 | async-start | bytes 2162688
  660.6 431.8 %reduce-scatter.24.cloned.1.call-start = ((), (), s32[]{:S(2)}) async-start(), calls=%async_computation.10 | async-start | bytes 2162688
  674.2 569.3 %reduce-scatter.22.cloned.1.call-start = ((), (), s32[]{:S(2)}) async-start(), calls=%async_computation.9 | async-start | bytes 2162688
  687.7 705.6 %reduce-scatter.18.cloned.1.call-start = ((), (), s32[]{:S(2)}) async-start(), calls=%async_computation.7 | async-start | bytes 1081344 | tf_op jit(solution)/shard_map/reduce_scatter | solution.py:160
Sparse Core Ops, SparseCore 0:
  14.5 42.6 reduce-scatter.19
  159.2 63.6 all-reduce.6
  225.2 142.5 all-gather.3
  647.2 143.1 reduce-scatter.27
  793.1 148.1 reduce-scatter.25
  944.2 148.1 reduce-scatter.23
  1095.2 148.2 reduce-scatter.21
  1247.0 146.2 reduce-scatter.17
where the time goes:
time: 1400 us
  waiting for transfers between devices  798 us (57%)
  blocking collectives  494 us (35%)
  local copies, waits for them, and re-layouts  61.1 us (4%)
  matrix products  21.8 us (2%)
  between operations  16.1 us (1%)
    unnamed x14, waiting for transfers between devices  648 us
    all_gather x5, blocking collectives, head_inputs(): everyone = lax.all_gather(mixed[..., inner_here:], 'tp', axis=2, tiled=True)  310 us
    reduce_scatter x1, waiting for transfers between devices, project_out(): lax.psum_scatter(partial_sums.astype(jnp.bfloat16), 'tp', scatter_dimensi...  148 us
    psum x1, blocking collectives, project_out(): totals = lax.psum(placed, 'tp')  135 us
    unnamed x51, local copies, waits for them, and re-layouts  51.4 us
  transfers between devices with their start and end apart: 9, of which 8 were waited for; matrix products, arithmetic and copies ran while one was open for 5% of the time, Pallas kernels for 0%

commit v1 on v0

v1 whole, which is shorter than its diff:
```python
import jax
import jax.numpy as jnp
from jax import lax
from jax.experimental import pallas as pl
from jax.experimental.pallas import tpu as pltpu
from jax.sharding import PartitionSpec as P

PROMPT = 256
FRESH = 64
ROWS = 320
PADDED = 384
WIDTH = 2048
CHANNELS = 256
BLOCK = 80
MSG = 336
MESH = pl.DeviceIdType.MESH
F32 = jnp.float32
BF16 = jnp.bfloat16
NT = (((1,), (1,)), ((), ()))


def mm(a, b):
    return jnp.dot(a, b, preferred_element_type=F32)


def mm_nt(a, b):
    return lax.dot_general(a, b, NT, preferred_element_type=F32)


def iota(shape, axis):
    return lax.broadcasted_iota(jnp.int32, shape, axis)


def silu(v):
    return v / (1.0 + jnp.exp(-v))


def kernel(
    prompt_ref, fresh_ref, in_ref, group_ref, out_ref,
    step_ref, taps_ref, bias_ref, group_taps_ref, group_bias_ref,
    step_bias_ref, decay_ref, skip_ref, gain_ref,
    prefill_ref, decode_ref,
    tokens, w_in, w_group, w_out, load_sem,
    packed_taps, a_src, a_dst, b_src, b_dst, maps, rs_src, rs_dst,
    mixed, gat, wide, sq_src, sq_dst, normed,
    d1_src, d1_dst, own, d2_src, d2_dst, d3_src, d3_dst,
    a_send, a_recv, b_send, b_recv, c_send, c_recv, rs_send, rs_recv,
    g_send, g_recv, q_send, q_recv, d1_send, d1_recv, d2_send, d2_recv, d3_send, d3_recv,
):
    rep = lax.axis_index("rep")
    samp = lax.axis_index("samp")
    tp = lax.axis_index("tp")
    low = tp // 8
    place = tp % 8
    across = place // 2
    core = place % 2
    group = tp // 4
    quarter = tp % 4

    def device(samp_index, tp_index):
        return (rep, samp_index, tp_index)

    barrier = pltpu.get_barrier_semaphore()

    def greet(samp_index, tp_index):
        pl.semaphore_signal(barrier, inc=1, device_id=device(samp_index, tp_index), device_id_type=MESH)

    for d in range(1, 4):
        greet((samp + d) % 4, tp)
        greet(samp, group * 4 + (quarter + d) % 4)
        greet(samp, low * 8 + ((across + d) % 4) * 2 + core)
    for i in range(8):
        @pl.when(quarter * 8 + i != tp)
        def _():
            greet(samp, quarter * 8 + i)
    for i in range(4):
        @pl.when(jnp.logical_or(low != samp, i != low))
        def _():
            greet(low, i * 8 + place)

    loads = [
        pltpu.make_async_copy(group_ref, w_group, load_sem.at[0]),
        pltpu.make_async_copy(prompt_ref, tokens.at[pl.ds(0, PROMPT)], load_sem.at[1]),
        pltpu.make_async_copy(fresh_ref, tokens.at[pl.ds(PROMPT, FRESH)], load_sem.at[2]),
        pltpu.make_async_copy(in_ref, w_in, load_sem.at[3]),
        pltpu.make_async_copy(out_ref, w_out, load_sem.at[4]),
    ]
    for load in loads:
        load.start()
    tokens[pl.ds(ROWS, PADDED - ROWS), :] = jnp.zeros((PADDED - ROWS, WIDTH), BF16)

    packed_taps[...] = jnp.zeros(packed_taps.shape, F32)
    for at, value in ((64, group_taps_ref[...]), (68, group_bias_ref[...])):
        high = value.astype(BF16).astype(F32)
        packed_taps[pl.ds(at, value.shape[0]), :] = high
        packed_taps[pl.ds(at + 8, value.shape[0]), :] = value - high

    row = iota((64, 64), 0)
    col = iota((64, 64), 1)
    regroup = (col == (row % 8) * 8 + row // 8).astype(F32).astype(BF16)
    requarter = (col == ((row % 16) // 4) * 16 + (row // 16) * 4 + row % 4).astype(F32).astype(BF16)

    for load in loads[:3]:
        load.wait()
    maps_partial = mm_nt(w_group[...], tokens[...]).astype(BF16)
    regrouped = mm(regroup, maps_partial)
    tail = regrouped[:, PROMPT:] + mm_nt(regroup, packed_taps[...].astype(BF16))
    a_src[:, :, pl.ds(0, PROMPT)] = regrouped[:, :PROMPT].reshape(8, 8, PROMPT).astype(BF16)
    a_src[:, :, pl.ds(PROMPT, 128)] = tail.reshape(8, 8, 128).astype(BF16)

    pl.semaphore_wait(
        barrier, 19 + jnp.where(quarter != low, 1, 0) + jnp.where(samp != low, 1, 0)
    )

    def a_copy(g):
        return pltpu.make_async_remote_copy(
            src_ref=a_src.at[g], dst_ref=a_dst.at[place],
            send_sem=a_send.at[g], recv_sem=a_recv.at[place],
            device_id=device(samp, g * 4 + low), device_id_type=MESH,
        )

    for g in range(8):
        @pl.when(g * 4 + low != tp)
        def _():
            a_copy(g).start()

        @pl.when(g * 4 + low == tp)
        def _():
            a_dst[pl.ds(place, 1)] = a_src[pl.ds(g, 1)]

    sizes = mm_nt(step_ref[...], tokens[...])
    loads[3].wait()
    gate_part = mm(tokens[pl.ds(0, ROWS), :], w_in[0])
    head_part = mm(tokens[pl.ds(0, ROWS), :], w_in[1])
    lane = iota((ROWS, 128), 1)
    size_row = iota((16, 128), 0)
    for h in range(4):
        gate_half = gate_part[:, 128 * (h // 2):128 * (h // 2) + 128]
        head_half = head_part[:, 128 * (h // 2):128 * (h // 2) + 128]
        if h % 2 == 0:
            both = jnp.where(lane < 64, gate_half, pltpu.roll(head_half, 64, 1))
        else:
            both = jnp.where(lane < 64, pltpu.roll(gate_half, 64, 1), head_half)
        rs_src[h, pl.ds(0, ROWS), :] = both.astype(BF16)
        piece = jnp.zeros((16, 128), F32)
        for b in range(3):
            piece = jnp.where(size_row == b, sizes[h:h + 1, 128 * b:128 * b + 128], piece)
        rs_src[h, pl.ds(ROWS, 16), :] = piece.astype(BF16)

    for i in range(8):
        @pl.when(quarter * 8 + i != tp)
        def _():
            pltpu.make_async_copy(a_dst.at[i], a_dst.at[i], a_recv.at[i]).wait()
    own_maps = a_dst[...].astype(F32).reshape(64, PADDED)
    b_src[...] = own_maps.astype(BF16)
    b_copies = [
        pltpu.make_async_remote_copy(
            src_ref=b_src, dst_ref=b_dst.at[d - 1],
            send_sem=b_send.at[d - 1], recv_sem=b_recv.at[d - 1],
            device_id=device((samp + d) % 4, tp), device_id_type=MESH,
        )
        for d in range(1, 4)
    ]
    for copy in b_copies:
        copy.start()
    rs_copies = [
        pltpu.make_async_remote_copy(
            src_ref=rs_src.at[(samp + d) % 4], dst_ref=rs_dst.at[d - 1],
            send_sem=rs_send.at[d - 1], recv_sem=rs_recv.at[d - 1],
            device_id=device((samp + d) % 4, tp), device_id_type=MESH,
        )
        for d in range(1, 4)
    ]
    for copy in rs_copies:
        copy.start()

    total = own_maps
    for d in range(3):
        b_copies[d].wait_recv()
        total = total + b_dst[d].astype(F32)
    total = total.astype(BF16).astype(F32)
    taps = [own_maps[:, 320 + k:321 + k] + own_maps[:, 328 + k:329 + k] for k in range(5)]
    before = total[:, :PROMPT]
    lane_p = iota((64, PROMPT), 1)
    conv = taps[4] + taps[3] * before
    for k in range(1, 4):
        conv = conv + taps[3 - k] * jnp.where(lane_p >= k, pltpu.roll(before, k, 1), 0.0)
    maps_prompt = silu(conv).astype(BF16)
    lane_f = iota((64, 128), 1)
    line = pltpu.roll(total[:, PROMPT:], 48, 1)
    for k in range(3):
        line = jnp.where(
            jnp.logical_and(lane_f >= 16 * k, lane_f < 16 * k + 16), before[:, 253 + k:254 + k], line
        )
    conv = taps[4] + taps[0] * line
    for k in range(1, 4):
        conv = conv + taps[k] * pltpu.roll(line, 128 - 16 * k, 1)
    maps_fresh = jnp.where(lane_f < 64, silu(conv), 0.0).astype(BF16)
    maps[quarter, :, pl.ds(0, PROMPT)] = maps_prompt
    maps[quarter, :, pl.ds(PROMPT, 128)] = maps_fresh
    c_copies = [
        pltpu.make_async_remote_copy(
            src_ref=maps.at[quarter], dst_ref=maps.at[quarter],
            send_sem=c_send.at[d - 1], recv_sem=c_recv.at[d - 1],
            device_id=device(samp, group * 4 + (quarter + d) % 4), device_id_type=MESH,
        )
        for d in range(1, 4)
    ]
    for copy in c_copies:
        copy.start()

    summed = rs_src[samp].astype(F32)
    for d in range(3):
        rs_copies[d].wait_recv()
        summed = summed + rs_dst[d].astype(F32)
    summed = summed.astype(BF16).astype(F32)
    lane128 = iota((1, 128), 1)

    def of_head(value):
        chosen = jnp.zeros((value.shape[0], 128), F32)
        for h in range(4):
            half = value[:, 128 * (h // 2):128 * (h // 2) + 128]
            if h % 2 == 0:
                half = pltpu.roll(half, 64, 1)
            chosen = jnp.where(samp == h, half, chosen)
        return jnp.where(lane128 >= 64, chosen, 0.0)

    taps8 = of_head(jnp.concatenate([taps_ref[...], bias_ref[...], jnp.zeros((3, CHANNELS), F32)], axis=0))
    before = summed[:PROMPT]
    row_p = iota((PROMPT, 128), 0)
    conv = taps8[4:5] + taps8[3:4] * before
    for k in range(1, 4):
        conv = conv + taps8[3 - k:4 - k] * jnp.where(row_p >= k, pltpu.roll(before, k, 0), 0.0)
    mixed[pl.ds(0, PROMPT), :] = silu(conv).astype(BF16)
    line = jnp.concatenate(
        [jnp.broadcast_to(before[253 + k:254 + k], (16, 128)) for k in range(3)] + [summed[PROMPT:ROWS]], axis=0
    )
    conv = taps8[4:5] + taps8[0:1] * line[0:64]
    for k in range(1, 4):
        conv = conv + taps8[k:k + 1] * line[16 * k:16 * k + 64]
    mixed[pl.ds(PROMPT, FRESH), :] = silu(conv).astype(BF16)
    mixed[pl.ds(ROWS, PADDED - ROWS), :] = jnp.zeros((PADDED - ROWS, 128), BF16)

    size = jnp.concatenate([summed[ROWS + b:ROWS + b + 1] for b in range(3)], axis=1)
    size = jnp.broadcast_to(size, (8, PADDED)) + step_bias_ref[samp]
    size = jnp.maximum(size, 0.0) + jnp.log1p(jnp.exp(-jnp.abs(size)))
    rate = jnp.exp(jnp.full((8, PADDED), decay_ref[samp], F32))
    logs = -size * rate
    run = logs[:, :PROMPT]
    lane_r = iota((8, PROMPT), 1)
    for k in (1, 2, 4, 8, 16, 32, 64, 128):
        run = run + jnp.where(lane_r >= k, pltpu.roll(run, k, 1), 0.0)
    run_f = logs[:, PROMPT:]
    lane_s = iota((8, 128), 1)
    for k in (16, 32):
        run_f = run_f + jnp.where(lane_s >= k, pltpu.roll(run_f, k, 1), 0.0)
    run_f = run_f + run[:, PROMPT - 1:PROMPT]
    runs = [run[0:1, 0:128], run[0:1, 128:256], run_f[0:1]]
    trail = jnp.concatenate([jnp.transpose(jnp.broadcast_to(r, (128, 128))) for r in runs], axis=0)[:ROWS]

    for copy in c_copies:
        copy.wait_recv()
    to_read = jnp.concatenate([maps[2], maps[3]], axis=0).astype(F32)
    readout = jnp.transpose(to_read)[:ROWS].astype(BF16)
    inputs = jnp.concatenate([maps[0], maps[1]], axis=0)
    row_q = iota((ROWS, 128), 0)
    reading = skip_ref[samp] * mixed[pl.ds(0, ROWS), :].astype(F32)
    for b in range(3):
        products = mm(readout, inputs[:, 128 * b:128 * b + 128])
        if b < 2:
            seen = lane + 128 * b <= row_q
        else:
            seen = jnp.logical_and(lane <= row_q - PROMPT, lane % 16 == row_q % 16)
        gap = jnp.where(seen, trail - runs[b], -1e30)
        weight = jnp.exp(gap) * size[0:1, 128 * b:128 * b + 128] * products
        reading = reading + mm(weight.astype(BF16), mixed[pl.ds(128 * b, 128), :])

    gate = pltpu.roll(summed[:ROWS], 64, 1)
    gated = reading * silu(gate)
    fresh = mm(requarter, gated[PROMPT:].astype(BF16))
    blocks = [jnp.concatenate([gated[64 * i:64 * i + 64], fresh[16 * i:16 * i + 16]], axis=0) for i in range(4)]
    upper = jnp.concatenate(blocks[:2], axis=0)
    lower = jnp.concatenate(blocks[2:], axis=0)
    lane_h = iota((160, 128), 1)
    gat[samp] = jnp.where(lane_h < 64, pltpu.roll(upper, 64, 1), lower).astype(BF16)
    g_copies = [
        pltpu.make_async_remote_copy(
            src_ref=gat.at[samp], dst_ref=gat.at[samp],
            send_sem=g_send.at[d - 1], recv_sem=g_recv.at[d - 1],
            device_id=device((samp + d) % 4, tp), device_id_type=MESH,
        )
        for d in range(1, 4)
    ]
    for copy in g_copies:
        copy.start()
    for copy in g_copies:
        copy.wait_recv()
    for pair in range(2):
        first, second = gat[2 * pair].astype(F32), gat[2 * pair + 1].astype(F32)
        columns = pl.ds(128 * pair, 128)
        wide[pl.ds(0, 160), columns] = jnp.where(lane_h < 64, first, pltpu.roll(second, 64, 1))
        wide[pl.ds(160, 160), columns] = jnp.where(lane_h < 64, pltpu.roll(first, 64, 1), second)

    squares = jnp.sum(wide[pl.ds(0, ROWS), :] * wide[pl.ds(0, ROWS), :], axis=1, keepdims=True)
    squares = jnp.concatenate([squares, jnp.zeros((PADDED - ROWS, 1), F32)], axis=0)
    squares = jnp.transpose(jnp.broadcast_to(squares, (PADDED, 128)))[0:8]
    sq_src[...] = squares
    q_copies = [
        pltpu.make_async_remote_copy(
            src_ref=sq_src, dst_ref=sq_dst.at[d - 1],
            send_sem=q_send.at[d - 1], recv_sem=q_recv.at[d - 1],
            device_id=device(samp, group * 4 + (quarter + d) % 4), device_id_type=MESH,
        )
        for d in range(1, 4)
    ]
    for copy in q_copies:
        copy.start()
    for d in range(3):
        q_copies[d].wait_recv()
        squares = squares + sq_dst[d]
    scale = lax.rsqrt(squares * (1.0 / 1024.0) + 1e-5)
    scale = jnp.transpose(jnp.broadcast_to(scale[0:1], (128, PADDED)))[:ROWS]
    for half in range(2):
        columns = pl.ds(128 * half, 128)
        normed[:, columns] = (wide[pl.ds(0, ROWS), columns] * scale * gain_ref[:, columns]).astype(BF16)

    loads[4].wait()

    def d1_copy(i):
        return pltpu.make_async_remote_copy(
            src_ref=d1_src.at[i], dst_ref=d1_dst.at[i],
            send_sem=d1_send.at[i], recv_sem=d1_recv.at[i],
            device_id=device(samp, low * 8 + across * 2 + 1 - core), device_id_type=MESH,
        )

    for i in range(4):
        columns = pl.ds(pl.multiple_of((2 * i + 1 - core) * 256, 256), 256)
        d1_src[i] = mm(normed[...], w_out[:, columns]).astype(BF16)
        d1_copy(i).start()
    for i in range(4):
        columns = pl.ds(pl.multiple_of((2 * i + core) * 256, 256), 256)
        own[i] = mm(normed[...], w_out[:, columns])
    for i in range(4):
        d1_copy(i).wait_recv()

    def d2_copy(d, s):
        return pltpu.make_async_remote_copy(
            src_ref=d2_src.at[d - 1, s], dst_ref=d2_dst.at[d - 1, s],
            send_sem=d2_send.at[d - 1, s], recv_sem=d2_recv.at[d - 1, s],
            device_id=device(samp, low * 8 + ((across + d) % 4) * 2 + core), device_id_type=MESH,
        )

    for s in range(4):
        rows = pl.ds(BLOCK * s, BLOCK)
        for d in range(1, 4):
            to = (across + d) % 4
            d2_src[d - 1, s] = (own[to, rows, :] + d1_dst[to, rows, :].astype(F32)).astype(BF16)
            d2_copy(d, s).start()

    def d3_copy(s):
        return pltpu.make_async_remote_copy(
            src_ref=d3_src.at[s], dst_ref=d3_dst.at[low],
            send_sem=d3_send.at[s], recv_sem=d3_recv.at[low],
            device_id=device(s, samp * 8 + place), device_id_type=MESH,
        )

    def stays(s):
        return jnp.logical_and(samp == low, samp == s)

    for s in range(4):
        rows = pl.ds(BLOCK * s, BLOCK)
        value = own[across, rows, :] + d1_dst[across, rows, :].astype(F32)
        for d in range(1, 4):
            d2_copy(d, s).wait_recv()
            value = value + d2_dst[d - 1, s].astype(F32)
        d3_src[s] = value.astype(BF16)

        @pl.when(stays(s))
        def _():
            d3_dst[low] = d3_src[s]

        @pl.when(jnp.logical_not(stays(s)))
        def _():
            d3_copy(s).start()

    for i in range(4):
        @pl.when(jnp.logical_or(low != samp, i != low))
        def _():
            pltpu.make_async_copy(d3_dst.at[i], d3_dst.at[i], d3_recv.at[i]).wait()
    value = d3_dst[0].astype(F32)
    for i in range(1, 4):
        value = value + d3_dst[i].astype(F32)
    prefill_ref[...] = value[:64].astype(BF16)
    decode_ref[...] = value[64:].astype(BF16)

    for g in range(8):
        @pl.when(g * 4 + low != tp)
        def _():
            a_copy(g).wait_send()
    for copy in b_copies + rs_copies + c_copies + g_copies + q_copies:
        copy.wait_send()
    for i in range(4):
        d1_copy(i).wait_send()
    for s in range(4):
        for d in range(1, 4):
            d2_copy(d, s).wait_send()

        @pl.when(jnp.logical_not(stays(s)))
        def _():
            d3_copy(s).wait_send()


def shards(
    prompt_tokens, step_tokens, lengths, input_weight, group_weight, step_weight,
    conv_weight, group_conv, conv_bias, group_bias, step_bias, decay_log, skip_gain, norm_gain, output_weight,
):
    anywhere = pl.BlockSpec(memory_space=pl.ANY)
    vector = pl.BlockSpec(memory_space=pltpu.VMEM)
    scalar = pl.BlockSpec(memory_space=pltpu.SMEM)
    dma = pltpu.SemaphoreType.DMA
    prefill, decode = pl.pallas_call(
        kernel,
        out_shape=(
            jax.ShapeDtypeStruct((64, CHANNELS), BF16),
            jax.ShapeDtypeStruct((16, CHANNELS), BF16),
        ),
        in_specs=[anywhere] * 5 + [vector] * 5 + [scalar] * 3 + [vector],
        out_specs=(vector, vector),
        scratch_shapes=[
            pltpu.VMEM((PADDED, WIDTH), BF16),
            pltpu.VMEM((2, WIDTH, CHANNELS), BF16),
            pltpu.VMEM((64, WIDTH), BF16),
            pltpu.VMEM((CHANNELS, WIDTH), BF16),
            dma((5,)),
            pltpu.VMEM((128, 64), F32),
            pltpu.VMEM((8, 8, PADDED), BF16),
            pltpu.VMEM((8, 8, PADDED), BF16),
            pltpu.VMEM((64, PADDED), BF16),
            pltpu.VMEM((3, 64, PADDED), BF16),
            pltpu.VMEM((4, 64, PADDED), BF16),
            pltpu.VMEM((4, MSG, 128), BF16),
            pltpu.VMEM((3, MSG, 128), BF16),
            pltpu.VMEM((PADDED, 128), BF16),
            pltpu.VMEM((4, 160, 128), BF16),
            pltpu.VMEM((ROWS, CHANNELS), F32),
            pltpu.VMEM((8, PADDED), F32),
            pltpu.VMEM((3, 8, PADDED), F32),
            pltpu.VMEM((ROWS, CHANNELS), BF16),
            pltpu.VMEM((4, ROWS, CHANNELS), BF16),
            pltpu.VMEM((4, ROWS, CHANNELS), BF16),
            pltpu.VMEM((4, ROWS, CHANNELS), F32),
            pltpu.VMEM((3, 4, BLOCK, CHANNELS), BF16),
            pltpu.VMEM((3, 4, BLOCK, CHANNELS), BF16),
            pltpu.VMEM((4, BLOCK, CHANNELS), BF16),
            pltpu.VMEM((4, BLOCK, CHANNELS), BF16),
            dma((8,)), dma((8,)), dma((3,)), dma((3,)), dma((3,)), dma((3,)), dma((3,)), dma((3,)),
            dma((3,)), dma((3,)), dma((3,)), dma((3,)), dma((4,)), dma((4,)),
            dma((3, 4)), dma((3, 4)), dma((4,)), dma((4,)),
        ],
        compiler_params=pltpu.CompilerParams(
            collective_id=0, has_side_effects=True, vmem_limit_bytes=40 * 1024 * 1024
        ),
        cost_estimate=pl.CostEstimate(flops=2 * 10**9, bytes_accessed=8 * 10**6, transcendentals=10**6),
    )(
        prompt_tokens.reshape(PROMPT, WIDTH),
        step_tokens.reshape(FRESH, WIDTH),
        input_weight,
        group_weight.T,
        output_weight,
        step_weight.T,
        conv_weight,
        conv_bias.reshape(1, CHANNELS),
        group_conv,
        group_bias.reshape(1, 64),
        step_bias,
        decay_log,
        skip_gain,
        norm_gain.reshape(1, CHANNELS),
    )
    active = jnp.arange(4)[:, None, None] < lengths[None]
    decode = decode.reshape(4, 4, 1, CHANNELS)
    return prefill.reshape(64, 1, CHANNELS), jnp.where(active[..., None], decode, jnp.zeros_like(decode))


def solution(mesh):
    placed = (
        P(None, "rep", "samp"),
        P(None, None, "rep", "samp"),
        P("samp", "rep"),
        P(None, "samp", "tp"),
        P("samp", "tp"),
        P("samp", "tp"),
        P(None, "tp"),
        P(None, "tp"),
        P("tp"),
        P("tp"),
        P("tp"),
        P("tp"),
        P("tp"),
        P("tp"),
        P("tp", "samp"),
    )
    return jax.shard_map(
        shards,
        mesh=mesh,
        in_specs=placed,
        out_specs=(P("samp", "rep", "tp"), P(None, "samp", "rep", "tp")),
        check_vma=False,
    )
```

time: 1400 us -> 94 us (0.07)
  waiting for transfers between devices: 798 us -> 0 us
  blocking collectives: 494 us -> 0 us
  Pallas kernels: 0 us -> 79.6 us
  local copies, waits for them, and re-layouts: 61.1 us -> 12.6 us
  matrix products: 21.8 us -> 0 us
  between operations: 16.1 us -> 0.68 us
    unnamed x14 -> x0, waiting for transfers between devices: 648 us -> none
    all_gather x6 -> x0, blocking collectives: 331 us -> none  [the longest x5 310 us: head_inputs(): everyone = lax.all_gather(mixed[..., inner_here:], 'tp', axis=2, tiled=True)]
    reduce_scatter x1 -> x0, waiting for transfers between devices: 148 us -> none  [project_out(): lax.psum_scatter(partial_sums.astype(jnp.bfloat16), 'tp', scatter_dimensi...]
    psum x1 -> x0, blocking collectives: 135 us -> none  [project_out(): totals = lax.psum(placed, 'tp')]
    pallas_call x0 -> x1, Pallas kernels: none -> 79.6 us  [shards(): pl.pallas_call(kernel, out_shape=(jax.ShapeDtypeStruct((64, CHANNELS), BF...]
    unnamed x51 -> x31, local copies, waits for them, and re-layouts: 51.4 us -> 12.6 us
    unnamed x1 -> x0, blocking collectives: 28 us -> none
    dot_general x12 -> x0, matrix products: 21.8 us -> none  [the longest x5 15.7 us: project_out(): jnp.einsum('sbi,id->sbd', normed, full_output, preferred_element_type=jnp...]
  transfers between devices with their start and end apart: 9 -> 0, of which waited for: 8 -> 0; matrix products, arithmetic and copies ran while one was open for 5% -> 0% of each run, Pallas kernels for 0% -> 0%
where the time goes in v1:
time: 94 us; the launch traced here: 93.5 us
  Pallas kernels  79.6 us (85%)
  local copies, waits for them, and re-layouts  12.6 us (13%)
    pallas_call x1, Pallas kernels, shards(): pl.pallas_call(kernel, out_shape=(jax.ShapeDtypeStruct((64, CHANNELS), BF...  79.6 us
    unnamed x31, local copies, waits for them, and re-layouts  12.6 us

profile of v1, /device:TPU:24, one launch (start us, length us, event | category | flops | bytes accessed | tf_op | source)
XLA Modules:
  0.0 93.5 jit_solution(3230866996940908413)
XLA Ops:
  0.6 0.0 copy-start
  0.6 1.6 %copy-done = bf16[2,2048,256]{2,1,0:T(8,128)(2,1)S(1)} copy-done((bf16[2,2048,256]{2,1,0:T(8,128)(2,1)S(1)}, bf16[2,2048,256]{2,1,0:T(8,128)(2,1)}, u32[]{:S(2)}) %copy-start) | copy-done | bytes 2097176
  2.2 0.0 copy-start.1
  2.2 1.2 %copy-done.1 = bf16[256,1,2048]{2,0,1:T(8,128)(2,1)S(1)} copy-done((bf16[256,1,2048]{2,0,1:T(8,128)(2,1)S(1)}, bf16[256,1,2048]{2,0,1:T(8,128)(2,1)}, u32[]{:S(2)}) %copy-start.1) | copy-done | bytes 1048600
  3.5 0.0 copy-start.2
  3.5 1.2 %copy-done.2 = bf16[256,2048]{1,0:T(8,128)(2,1)S(1)} copy-done((bf16[256,2048]{1,0:T(8,128)(2,1)S(1)}, bf16[256,2048]{1,0:T(8,128)(2,1)}, u32[]{:S(2)}) %copy-start.2) | copy-done | bytes 1048600
  4.7 0.0 copy-start.3
  4.7 0.9 %copy-done.3 = bf16[4,16,1,2048]{3,1,2,0:T(8,128)(2,1)S(1)} copy-done((bf16[4,16,1,2048]{3,1,2,0:T(8,128)(2,1)S(1)}, bf16[4,16,1,2048]{3,1,2,0:T(8,128)(2,1)}, u32[]{:S(2)}) %copy-start.3) | copy-done | bytes 262168
  5.6 0.0 copy-start.4
  5.6 0.9 %copy-done.4 = bf16[2048,64]{0,1:T(8,128)(2,1)S(1)} copy-done((bf16[2048,64]{0,1:T(8,128)(2,1)S(1)}, bf16[2048,64]{0,1:T(8,128)(2,1)}, u32[]{:S(2)}) %copy-start.4) | copy-done | bytes 262168
  6.6 0.0 copy-start.5
  6.6 0.7 copy-done.5
  7.3 0.0 copy-start.6
  7.3 0.7 copy-done.6
  8.0 0.0 copy-start.7
  8.0 0.7 copy-done.7
  8.7 0.0 copy-start.8
  8.7 0.7 copy-done.8
  9.3 0.0 copy-start.9
  9.3 0.7 copy-done.9
  10.0 0.0 copy-start.10
  10.0 0.7 copy-done.10
  10.7 0.0 copy-start.11
  10.7 0.7 copy-done.11
  11.3 0.0 copy-start.12
  11.3 0.7 copy-done.12
  12.0 0.0 copy-start.13
  12.0 0.7 copy-done.13
  12.6 0.0 copy-start.14
  12.7 79.6 %shard_map.158 = (bf16[64,256]{1,0:T(8,128)(2,1)S(1)}, bf16[16,256]{1,0:T(8,128)(2,1)S(1)}) custom-call(bf16[256,2048]{1,0:T(8,128)(2,1)S(1)} %bitcast.12, bf16[64,2048]{1,0:T(8,128)(2,1)S(1)} %bitcast.13, bf16[2,2048,256]{2,1,0:T(8,128)(2,1)S(1)} %copy-done, bf16[64,2048]{1,0:T(8,128)(2,1)S(1)} %bitcast.14, bf16[256,2048]{1,0:T(8,128)(2,1)S(1)} %copy-done.2, ...), custom_call_target="tpu_custom_call" | custom-call | flops 2000000000 | bytes 8000000 | tf_op jit(solution)/shard_map/pallas_call | solution.py:421
  92.2 0.0 copy-done.14
  92.2 0.7 bitcast_select_fusion
  92.9 0.6 copy.19
  (2 shorter events, 0.0 us)
Async XLA Ops:
  0.6 1.6 %copy-start = (bf16[2,2048,256]{2,1,0:T(8,128)(2,1)S(1)}, bf16[2,2048,256]{2,1,0:T(8,128)(2,1)}, u32[]{:S(2)}) copy-start(bf16[2,2048,256]{2,1,0:T(8,128)(2,1)} %in_ref.1) | copy-start | bytes 6291460
  2.2 1.2 %copy-start.1 = (bf16[256,1,2048]{2,0,1:T(8,128)(2,1)S(1)}, bf16[256,1,2048]{2,0,1:T(8,128)(2,1)}, u32[]{:S(2)}) copy-start(bf16[256,1,2048]{2,0,1:T(8,128)(2,1)} %param.15) | copy-start | bytes 3145732
  3.5 1.2 %copy-start.2 = (bf16[256,2048]{1,0:T(8,128)(2,1)S(1)}, bf16[256,2048]{1,0:T(8,128)(2,1)}, u32[]{:S(2)}) copy-start(bf16[256,2048]{1,0:T(8,128)(2,1)} %out_ref.1) | copy-start | bytes 3145732
  4.7 0.9 %copy-start.3 = (bf16[4,16,1,2048]{3,1,2,0:T(8,128)(2,1)S(1)}, bf16[4,16,1,2048]{3,1,2,0:T(8,128)(2,1)}, u32[]{:S(2)}) copy-start(bf16[4,16,1,2048]{3,1,2,0:T(8,128)(2,1)} %param.16) | copy-start | bytes 786436
  5.6 0.9 %copy-start.4 = (bf16[2048,64]{0,1:T(8,128)(2,1)S(1)}, bf16[2048,64]{0,1:T(8,128)(2,1)}, u32[]{:S(2)}) copy-start(bf16[2048,64]{0,1:T(8,128)(2,1)} %param.19) | copy-start | bytes 786436
  6.6 0.7 copy-start.5
  7.3 0.7 copy-start.6
  8.0 0.7 copy-start.7
  8.7 0.7 copy-start.8
  9.3 0.7 copy-start.9
  10.0 0.7 copy-start.10
  10.7 0.7 copy-start.11
  11.3 0.7 copy-start.12
  12.0 0.7 copy-start.13
  12.6 79.6 %copy-start.14 = (s32[4,1]{0,1:T(1,128)S(1)}, s32[4,1]{0,1:T(1,128)}, u32[]{:S(2)}) copy-start(s32[4,1]{0,1:T(1,128)} %param.17) | copy-start | bytes 52

commit v2 on v1

v2 whole, which is shorter than its diff:
```python
import jax
import jax.numpy as jnp
from jax import lax
from jax.experimental import pallas as pl
from jax.experimental.pallas import tpu as pltpu
from jax.sharding import PartitionSpec as P

PROMPT = 256
FRESH = 64
ROWS = 320
PADDED = 384
WIDTH = 2048
CHANNELS = 256
BLOCK = 80
VMEM_LIMIT = 60 * 1024 * 1024
MESH = pl.DeviceIdType.MESH
F32 = jnp.float32
BF16 = jnp.bfloat16
NT = (((1,), (1,)), ((), ()))


def mm(a, b):
    return jnp.dot(a, b, preferred_element_type=F32)


def mm_nt(a, b):
    return lax.dot_general(a, b, NT, preferred_element_type=F32)


def iota(shape, axis):
    return lax.broadcasted_iota(jnp.int32, shape, axis)


def silu(v):
    return v / (1.0 + jnp.exp(-v))


def kernel(
    prompt_ref, fresh_ref, in_ref, group_ref, out_ref, step_ref, taps_ref, bias_ref,
    group_taps_ref, group_bias_ref, step_bias_ref, decay_ref, skip_ref, gain_ref,
    prefill_ref, decode_ref,
    tokens, w_in, w_group, w_out, w_step, taps_v, bias_v, group_taps_v, group_bias_v,
    step_bias_v, decay_v, skip_v, gain_v, load_sem,
    packed_taps, a_src, a_dst, b_src, b_dst, maps, x_src, x_dst, z_src, z_dst,
    mixed, weights, gat, wide, sq_src, sq_dst, unscaled,
    d1_src, d1_dst, own, d2_src, d2_dst, d3_src, d3_dst,
    a_send, a_recv, b_send, b_recv, c_send, c_recv, x_send, x_recv, z_send, z_recv,
    g_send, g_recv, q_send, q_recv, d1_send, d1_recv, d2_send, d2_recv, d3_send, d3_recv,
):
    rep = lax.axis_index("rep")
    samp = lax.axis_index("samp")
    tp = lax.axis_index("tp")
    low = tp // 8
    place = tp % 8
    across = place // 2
    core = place % 2
    group = tp // 4
    quarter = tp % 4

    def device(samp_index, tp_index):
        return (rep, samp_index, tp_index)

    barrier = pltpu.get_barrier_semaphore()

    def greet(samp_index, tp_index):
        pl.semaphore_signal(barrier, inc=1, device_id=device(samp_index, tp_index), device_id_type=MESH)

    for d in (2, 1, 3):
        greet((samp + d) % 4, tp)
    for i in range(4):
        @pl.when(jnp.logical_or(low != samp, i != low))
        def _():
            greet(low, i * 8 + place)
    for i in range(8):
        @pl.when(quarter * 8 + i != tp)
        def _():
            greet(samp, quarter * 8 + i)
    for d in range(1, 4):
        greet(samp, group * 4 + (quarter + d) % 4)
        greet(samp, low * 8 + ((across + d) % 4) * 2 + core)

    pairs = (
        (group_ref, w_group), (prompt_ref, tokens.at[pl.ds(0, PROMPT)]), (fresh_ref, tokens.at[pl.ds(PROMPT, FRESH)]),
        (group_taps_ref, group_taps_v), (group_bias_ref, group_bias_v), (step_ref, w_step),
        (in_ref.at[1], w_in.at[1]), (in_ref.at[0], w_in.at[0]), (taps_ref, taps_v), (bias_ref, bias_v),
        (step_bias_ref, step_bias_v), (decay_ref, decay_v), (skip_ref, skip_v), (gain_ref, gain_v), (out_ref, w_out),
    )
    loads = [pltpu.make_async_copy(a, b, load_sem.at[i]) for i, (a, b) in enumerate(pairs)]
    for load in loads:
        load.start()
    sends = []

    def copy(source, target, send, recv, samp_index, tp_index):
        return pltpu.make_async_remote_copy(
            src_ref=source, dst_ref=target, send_sem=send, recv_sem=recv,
            device_id=device(samp_index, tp_index), device_id_type=MESH,
        )

    def start(copies):
        for one in copies:
            one.start()
            sends.append(one)
        return copies

    tokens[pl.ds(ROWS, PADDED - ROWS), :] = jnp.zeros((PADDED - ROWS, WIDTH), BF16)
    packed_taps[...] = jnp.zeros(packed_taps.shape, F32)
    mixed[pl.ds(ROWS, PADDED - ROWS), :] = jnp.zeros((PADDED - ROWS, 128), BF16)

    row = iota((64, 64), 0)
    col = iota((64, 64), 1)
    regroup = (col == (row % 8) * 8 + row // 8).astype(F32).astype(BF16)
    requarter = (col == ((row % 16) // 4) * 16 + (row // 16) * 4 + row % 4).astype(F32).astype(BF16)

    for load in loads[:5]:
        load.wait()
    for at, value in ((64, group_taps_v[...]), (68, group_bias_v[...])):
        high = value.astype(BF16).astype(F32)
        packed_taps[pl.ds(at, value.shape[0]), :] = high
        packed_taps[pl.ds(at + 8, value.shape[0]), :] = value - high
    maps_partial = mm_nt(w_group[...], tokens[...]).astype(BF16)
    regrouped = mm(regroup, maps_partial)
    tail = regrouped[:, PROMPT:] + mm_nt(regroup, packed_taps[...].astype(BF16))
    a_src[:, :, pl.ds(0, PROMPT)] = regrouped[:, :PROMPT].reshape(8, 8, PROMPT).astype(BF16)
    a_src[:, :, pl.ds(PROMPT, 128)] = tail.reshape(8, 8, 128).astype(BF16)

    pl.semaphore_wait(
        barrier, 19 + jnp.where(quarter != low, 1, 0) + jnp.where(samp != low, 1, 0)
    )

    def a_copy(g):
        return copy(a_src.at[g], a_dst.at[place], a_send.at[g], a_recv.at[place], samp, g * 4 + low)

    for g in range(8):
        @pl.when(g * 4 + low != tp)
        def _():
            a_copy(g).start()

        @pl.when(g * 4 + low == tp)
        def _():
            a_dst[pl.ds(place, 1)] = a_src[pl.ds(g, 1)]

    lane_h = iota((160, 128), 1)

    def packed(part, h):
        upper = part[:160, 128 * (h // 2):128 * (h // 2) + 128]
        lower = part[160:, 128 * (h // 2):128 * (h // 2) + 128]
        if h % 2 == 0:
            return jnp.where(lane_h < 64, upper, pltpu.roll(lower, 64, 1)).astype(BF16)
        return jnp.where(lane_h < 64, pltpu.roll(upper, 64, 1), lower).astype(BF16)

    def to_heads(source, target, send, recv):
        return [
            copy(source.at[(samp + d) % 4], target.at[d - 1], send.at[d - 1], recv.at[d - 1], (samp + d) % 4, tp)
            for d in (2, 1, 3)
        ]

    loads[5].wait()
    sizes = mm_nt(w_step[...], tokens[...])
    loads[6].wait()
    head_part = mm(tokens[pl.ds(0, ROWS), :], w_in[1])
    size_row = iota((16, 128), 0)
    for h in range(4):
        x_src[h, pl.ds(0, 160), :] = packed(head_part, h)
        piece = jnp.zeros((16, 128), F32)
        for b in range(3):
            piece = jnp.where(size_row == b, sizes[h:h + 1, 128 * b:128 * b + 128], piece)
        x_src[h, pl.ds(160, 16), :] = piece.astype(BF16)
    x_copies = start(to_heads(x_src, x_dst, x_send, x_recv))
    loads[7].wait()
    gate_part = mm(tokens[pl.ds(0, ROWS), :], w_in[0])
    for h in range(4):
        z_src[h] = packed(gate_part, h)

    for i in range(8):
        @pl.when(quarter * 8 + i != tp)
        def _():
            pltpu.make_async_copy(a_dst.at[i], a_dst.at[i], a_recv.at[i]).wait()
    own_maps = a_dst[...].astype(F32).reshape(64, PADDED)
    lane_q = iota((32, 128), 1)
    fresh_maps = own_maps[:, PROMPT:]
    b_src[pl.ds(0, 64), :] = own_maps[:, 0:128].astype(BF16)
    b_src[pl.ds(64, 64), :] = own_maps[:, 128:256].astype(BF16)
    b_src[pl.ds(128, 32), :] = jnp.where(lane_q < 64, fresh_maps[:32], pltpu.roll(fresh_maps[32:], 64, 1)).astype(BF16)
    b_copies = start([
        copy(b_src, b_dst.at[d - 1], b_send.at[d - 1], b_recv.at[d - 1], (samp + d) % 4, tp) for d in (2, 1, 3)
    ])
    for one in b_copies:
        one.wait_send()
    z_copies = start(to_heads(z_src, z_dst, z_send, z_recv))

    lane128 = iota((1, 128), 1)

    def of_head(value):
        chosen = jnp.zeros((value.shape[0], 128), F32)
        for h in range(4):
            half = value[:, 128 * (h // 2):128 * (h // 2) + 128]
            if h % 2 == 0:
                half = pltpu.roll(half, 64, 1)
            chosen = jnp.where(samp == h, half, chosen)
        return jnp.where(lane128 >= 64, chosen, 0.0)

    def own_scalar(ref):
        return jnp.sum(jnp.where(iota((1, 4), 1) == samp, ref[...], 0.0), axis=1, keepdims=True)

    def unpacked(value):
        return jnp.concatenate([pltpu.roll(value, 64, 1), value], axis=0)

    for load in loads[8:13]:
        load.wait()
    taps8 = of_head(jnp.concatenate([taps_v[...], bias_v[...], jnp.zeros((3, CHANNELS), F32)], axis=0))
    skip = own_scalar(skip_v)
    step_bias = own_scalar(step_bias_v)
    rate = jnp.exp(own_scalar(decay_v))
    for one in x_copies:
        one.wait_recv()
    summed = x_src[samp].astype(F32)
    for d in range(3):
        summed = summed + x_dst[d].astype(F32)
    summed = summed.astype(BF16).astype(F32)
    heads = unpacked(summed[:160])
    before = heads[:PROMPT]
    row_p = iota((PROMPT, 128), 0)
    conv = taps8[4:5] + taps8[3:4] * before
    for k in range(1, 4):
        conv = conv + taps8[3 - k:4 - k] * jnp.where(row_p >= k, pltpu.roll(before, k, 0), 0.0)
    mixed[pl.ds(0, PROMPT), :] = silu(conv).astype(BF16)
    line = jnp.concatenate(
        [jnp.broadcast_to(before[253 + k:254 + k], (16, 128)) for k in range(3)] + [heads[PROMPT:ROWS]], axis=0
    )
    conv = taps8[4:5] + taps8[0:1] * line[0:64]
    for k in range(1, 4):
        conv = conv + taps8[k:k + 1] * line[16 * k:16 * k + 64]
    mixed[pl.ds(PROMPT, FRESH), :] = silu(conv).astype(BF16)

    size = jnp.concatenate([summed[160 + b:161 + b] for b in range(3)], axis=1)
    size = jnp.broadcast_to(size, (8, PADDED)) + step_bias
    size = jnp.maximum(size, 0.0) + jnp.log1p(jnp.exp(-jnp.abs(size)))
    logs = -size * rate
    run = logs[:, :PROMPT]
    lane_r = iota((8, PROMPT), 1)
    for k in (1, 2, 4, 8, 16, 32, 64, 128):
        run = run + jnp.where(lane_r >= k, pltpu.roll(run, k, 1), 0.0)
    run_f = logs[:, PROMPT:]
    lane_s = iota((8, 128), 1)
    for k in (16, 32):
        run_f = run_f + jnp.where(lane_s >= k, pltpu.roll(run_f, k, 1), 0.0)
    run_f = run_f + run[:, PROMPT - 1:PROMPT]
    runs = [run[0:1, 0:128], run[0:1, 128:256], run_f[0:1]]
    trail = jnp.concatenate([jnp.transpose(jnp.broadcast_to(r, (128, 128))) for r in runs], axis=0)[:ROWS]
    lane = iota((128, 128), 1)
    row_q = iota((128, 128), 0)
    tiles = ((256, 64, 0), (256, 64, 1), (256, 64, 2), (0, 128, 0), (128, 128, 0), (128, 128, 1))
    offsets = (0, 64, 128, 192, 320, 448)
    for (first, count, b), offset in zip(tiles, offsets):
        gap = trail[first:first + count] - runs[b]
        if b == 2:
            seen = jnp.logical_and(lane <= row_q, lane % 16 == row_q % 16)[:count]
            gap = jnp.where(seen, gap, -1e30)
        elif first == 128 * b:
            gap = jnp.where(lane <= row_q, gap, -1e30)
        weights[pl.ds(offset, count), :] = jnp.exp(gap) * size[0:1, 128 * b:128 * b + 128]

    for one in b_copies:
        one.wait_recv()
    total = b_src[...].astype(F32)
    for d in range(3):
        total = total + b_dst[d].astype(F32)
    total = total.astype(BF16).astype(F32)
    taps = [own_maps[:, 320 + k:321 + k] + own_maps[:, 328 + k:329 + k] for k in range(5)]
    before = jnp.concatenate([total[0:64], total[64:128]], axis=1)
    lane_p = iota((64, PROMPT), 1)
    conv = taps[4] + taps[3] * before
    for k in range(1, 4):
        conv = conv + taps[3 - k] * jnp.where(lane_p >= k, pltpu.roll(before, k, 1), 0.0)
    maps_prompt = silu(conv).astype(BF16)
    lane_f = iota((64, 128), 1)
    line = jnp.concatenate([total[128:160], pltpu.roll(total[128:160], 64, 1)], axis=0)
    line = pltpu.roll(line, 48, 1)
    for k in range(3):
        line = jnp.where(
            jnp.logical_and(lane_f >= 16 * k, lane_f < 16 * k + 16), before[:, 253 + k:254 + k], line
        )
    conv = taps[4] + taps[0] * line
    for k in range(1, 4):
        conv = conv + taps[k] * pltpu.roll(line, 128 - 16 * k, 1)
    maps_fresh = jnp.where(lane_f < 64, silu(conv), 0.0).astype(BF16)
    maps[quarter, :, pl.ds(0, PROMPT)] = maps_prompt
    maps[quarter, :, pl.ds(PROMPT, 128)] = maps_fresh
    c_copies = start([
        copy(maps.at[quarter], maps.at[quarter], c_send.at[d - 1], c_recv.at[d - 1], samp, group * 4 + (quarter + d) % 4)
        for d in (3, 2, 1)
    ])
    for one in c_copies:
        one.wait_recv()
    inputs = jnp.concatenate([maps[0], maps[1]], axis=0)
    to_read = jnp.concatenate([maps[2], maps[3]], axis=0).astype(F32)
    readout = jnp.transpose(to_read).astype(BF16)

    def read(first, count, blocks):
        value = skip * mixed[pl.ds(first, count), :].astype(F32)
        for b, offset in blocks:
            products = mm(readout[first:first + count], inputs[:, 128 * b:128 * b + 128])
            seen = (weights[pl.ds(offset, count), :] * products).astype(BF16)
            value = value + mm(seen, mixed[pl.ds(128 * b, 128), :])
        return value

    fresh = read(256, 64, ((0, 0), (1, 64), (2, 128)))
    halves = [read(0, 128, ((0, 192),)), read(128, 128, ((0, 320), (1, 448)))]
    for one in z_copies:
        one.wait_recv()
    gate = z_src[samp].astype(F32)
    for d in range(3):
        gate = gate + z_dst[d].astype(F32)
    gate = silu(unpacked(gate.astype(BF16).astype(F32)))
    fresh = mm(requarter, (fresh * gate[PROMPT:]).astype(BF16))

    lane_c = iota((BLOCK, 128), 1)
    g_copies = []
    for c in range(2):
        gated = halves[c] * gate[128 * c:128 * c + 128]
        upper = jnp.concatenate([gated[:64], fresh[32 * c:32 * c + 16]], axis=0)
        lower = jnp.concatenate([gated[64:], fresh[32 * c + 16:32 * c + 32]], axis=0)
        gat[c, samp] = jnp.where(lane_c < 64, pltpu.roll(upper, 64, 1), lower).astype(BF16)
        g_copies.append(start([
            copy(gat.at[c, samp], gat.at[c, samp], g_send.at[c, d - 1], g_recv.at[c, d - 1], (samp + d) % 4, tp)
            for d in (2, 1, 3)
        ]))

    for load in loads[13:]:
        load.wait()

    def d1_copy(c, i):
        return copy(
            d1_src.at[c, i], d1_dst.at[c, i], d1_send.at[c, i], d1_recv.at[c, i],
            samp, low * 8 + across * 2 + 1 - core,
        )

    def d2_copy(d, s):
        return copy(
            d2_src.at[d - 1, s], d2_dst.at[d - 1, s], d2_send.at[d - 1, s], d2_recv.at[d - 1, s],
            samp, low * 8 + ((across + d) % 4) * 2 + core,
        )

    def d3_copy(s):
        return copy(d3_src.at[s], d3_dst.at[low], d3_send.at[s], d3_recv.at[low], s, samp * 8 + place)

    for c in range(2):
        for one in g_copies[c]:
            one.wait_recv()
        for pair in range(2):
            first, second = gat[c, 2 * pair].astype(F32), gat[c, 2 * pair + 1].astype(F32)
            columns = pl.ds(128 * pair, 128)
            wide[pl.ds(0, BLOCK), columns] = jnp.where(lane_c < 64, first, pltpu.roll(second, 64, 1))
            wide[pl.ds(BLOCK, BLOCK), columns] = jnp.where(lane_c < 64, pltpu.roll(first, 64, 1), second)
        gathered = wide[...]
        unscaled[...] = (gathered * gain_v[...]).astype(BF16)

        squares = jnp.sum(gathered * gathered, axis=1, keepdims=True)
        squares = jnp.concatenate([squares, jnp.zeros((96, 1), F32)], axis=0)
        squares = jnp.transpose(jnp.broadcast_to(squares, (256, 128)))[0:8]
        sq_src[c] = squares
        q_copies = start([
            copy(
                sq_src.at[c], sq_dst.at[c, d - 1], q_send.at[c, d - 1], q_recv.at[c, d - 1],
                samp, group * 4 + (quarter + d) % 4,
            )
            for d in (3, 2, 1)
        ])

        d1_copies = [d1_copy(c, i) for i in range(4)]
        for i in range(4):
            columns = pl.ds(pl.multiple_of((2 * i + 1 - core) * 256, 256), 256)
            d1_src[c, i] = mm(unscaled[...], w_out[:, columns]).astype(BF16)
            start([d1_copies[i]])
        for i in range(4):
            columns = pl.ds(pl.multiple_of((2 * i + core) * 256, 256), 256)
            own[i] = mm(unscaled[...], w_out[:, columns])
        for one in q_copies:
            one.wait_recv()
        for d in range(3):
            squares = squares + sq_dst[c, d]
        scale = lax.rsqrt(squares * (1.0 / 1024.0) + 1e-5)
        scale = jnp.transpose(jnp.broadcast_to(scale[0:1], (128, 256)))[:160]
        scale = jnp.concatenate([scale, scale], axis=1)
        for one in d1_copies:
            one.wait_recv()
        for half in range(2):
            s = 2 * c + half
            rows = pl.ds(BLOCK * half, BLOCK)
            by = scale[BLOCK * half:BLOCK * half + BLOCK]
            for d in (2, 1, 3):
                to = (across + d) % 4
                d2_src[d - 1, s] = ((own[to, rows, :] + d1_dst[c, to, rows, :].astype(F32)) * by).astype(BF16)
                start([d2_copy(d, s)])
            kept = (own[across, rows, :] + d1_dst[c, across, rows, :].astype(F32)) * by
            if s == 0:
                kept_all = [kept]
            else:
                kept_all.append(kept)

    def stays(s):
        return jnp.logical_and(samp == low, samp == s)

    for s in range(4):
        value = kept_all[s]
        for d in range(1, 4):
            d2_copy(d, s).wait_recv()
            value = value + d2_dst[d - 1, s].astype(F32)
        d3_src[s] = value.astype(BF16)

        @pl.when(stays(s))
        def _():
            d3_dst[low] = d3_src[s]

        @pl.when(jnp.logical_not(stays(s)))
        def _():
            d3_copy(s).start()

    for i in range(4):
        @pl.when(jnp.logical_or(low != samp, i != low))
        def _():
            pltpu.make_async_copy(d3_dst.at[i], d3_dst.at[i], d3_recv.at[i]).wait()
    value = d3_dst[0].astype(F32)
    for i in range(1, 4):
        value = value + d3_dst[i].astype(F32)
    prefill_ref[...] = value[:64].astype(BF16)
    decode_ref[...] = value[64:].astype(BF16)

    for g in range(8):
        @pl.when(g * 4 + low != tp)
        def _():
            a_copy(g).wait_send()
    for one in sends:
        if not any(one is other for other in b_copies):
            one.wait_send()
    for s in range(4):
        @pl.when(jnp.logical_not(stays(s)))
        def _():
            d3_copy(s).wait_send()


def shards(
    prompt_tokens, step_tokens, lengths, input_weight, group_weight, step_weight,
    conv_weight, group_conv, conv_bias, group_bias, step_bias, decay_log, skip_gain, norm_gain, output_weight,
):
    anywhere = pl.BlockSpec(memory_space=pl.ANY)
    vector = pl.BlockSpec(memory_space=pltpu.VMEM)

    def dma(*shape):
        return pltpu.SemaphoreType.DMA(shape)

    def room(*shape):
        return pltpu.VMEM(shape, BF16)

    def wide_room(*shape):
        return pltpu.VMEM(shape, F32)

    prefill, decode = pl.pallas_call(
        kernel,
        out_shape=(
            jax.ShapeDtypeStruct((64, CHANNELS), BF16),
            jax.ShapeDtypeStruct((16, CHANNELS), BF16),
        ),
        in_specs=[anywhere] * 14,
        out_specs=(vector, vector),
        scratch_shapes=[
            room(PADDED, WIDTH), room(2, WIDTH, CHANNELS), room(64, WIDTH), room(CHANNELS, WIDTH), room(4, WIDTH),
            wide_room(4, CHANNELS), wide_room(1, CHANNELS), wide_room(4, 64), wide_room(1, 64),
            wide_room(1, 4), wide_room(1, 4), wide_room(1, 4), wide_room(1, CHANNELS), dma(15),
            wide_room(128, 64),
            room(8, 8, PADDED), room(8, 8, PADDED),
            room(160, 128), room(3, 160, 128),
            room(4, 64, PADDED),
            room(4, 176, 128), room(3, 176, 128),
            room(4, 160, 128), room(3, 160, 128),
            room(PADDED, 128), wide_room(576, 128),
            room(2, 4, BLOCK, 128), wide_room(2 * BLOCK, CHANNELS),
            wide_room(2, 8, 256), wide_room(2, 3, 8, 256),
            room(2 * BLOCK, CHANNELS),
            room(2, 4, 2 * BLOCK, CHANNELS), room(2, 4, 2 * BLOCK, CHANNELS), wide_room(4, 2 * BLOCK, CHANNELS),
            room(3, 4, BLOCK, CHANNELS), room(3, 4, BLOCK, CHANNELS),
            room(4, BLOCK, CHANNELS), room(4, BLOCK, CHANNELS),
            dma(8), dma(8), dma(3), dma(3), dma(3), dma(3), dma(3), dma(3), dma(3), dma(3),
            dma(2, 3), dma(2, 3), dma(2, 3), dma(2, 3), dma(2, 4), dma(2, 4), dma(3, 4), dma(3, 4), dma(4), dma(4),
        ],
        compiler_params=pltpu.CompilerParams(
            collective_id=0, has_side_effects=True, vmem_limit_bytes=VMEM_LIMIT
        ),
        cost_estimate=pl.CostEstimate(flops=2 * 10**9, bytes_accessed=8 * 10**6, transcendentals=10**6),
    )(
        prompt_tokens.reshape(PROMPT, WIDTH),
        step_tokens.reshape(FRESH, WIDTH),
        input_weight,
        group_weight.T,
        output_weight,
        step_weight.T,
        conv_weight,
        conv_bias.reshape(1, CHANNELS),
        group_conv,
        group_bias.reshape(1, 64),
        step_bias.reshape(1, 4),
        decay_log.reshape(1, 4),
        skip_gain.reshape(1, 4),
        norm_gain.reshape(1, CHANNELS),
    )
    active = jnp.arange(4)[:, None, None] < lengths[None]
    decode = decode.reshape(4, 4, 1, CHANNELS)
    return prefill.reshape(64, 1, CHANNELS), jnp.where(active[..., None], decode, jnp.zeros_like(decode))


def solution(mesh):
    placed = (
        P(None, "rep", "samp"),
        P(None, None, "rep", "samp"),
        P("samp", "rep"),
        P(None, "samp", "tp"),
        P("samp", "tp"),
        P("samp", "tp"),
        P(None, "tp"),
        P(None, "tp"),
        P("tp"),
        P("tp"),
        P("tp"),
        P("tp"),
        P("tp"),
        P("tp"),
        P("tp", "samp"),
    )
    return jax.shard_map(
        shards,
        mesh=mesh,
        in_specs=placed,
        out_specs=(P("samp", "rep", "tp"), P(None, "samp", "rep", "tp")),
        check_vma=False,
    )
```

time: 94 us -> 77.6 us (0.83)
  local copies, waits for them, and re-layouts: 12.6 us -> 2.09 us
  Pallas kernels: 79.6 us -> 73.8 us
    unnamed x31 -> x3, local copies, waits for them, and re-layouts: 12.6 us -> 1.38 us
    pallas_call x1, Pallas kernels: 79.6 us -> 73.8 us  [shards(): pl.pallas_call(kernel, out_shape=(jax.ShapeDtypeStruct((64, CHANNELS), BF...]
where the time goes in v2:
time: 77.6 us; the launch traced here: 77.2 us
  Pallas kernels  73.8 us (95%)
  local copies, waits for them, and re-layouts  2.09 us (3%)
    pallas_call x1, Pallas kernels, shards(): pl.pallas_call(kernel, out_shape=(jax.ShapeDtypeStruct((64, CHANNELS), BF...  73.8 us

profile of v2, /device:TPU:24, one launch (start us, length us, event | category | flops | bytes accessed | tf_op | source)
XLA Modules:
  0.0 77.2 jit_solution(152995046103439051)
XLA Ops:
  0.6 0.0 copy-start
  0.6 73.8 %shard_map.158 = (bf16[64,256]{1,0:T(8,128)(2,1)}, bf16[16,256]{1,0:T(8,128)(2,1)}) custom-call(bf16[256,2048]{1,0:T(8,128)(2,1)} %bitcast.15, bf16[64,2048]{1,0:T(8,128)(2,1)} %bitcast.16, bf16[2,2048,256]{2,1,0:T(8,128)(2,1)} %in_ref.1, bf16[64,2048]{1,0:T(8,128)(2,1)} %bitcast.17, bf16[256,2048]{1,0:T(8,128)(2,1)} %out_ref.1, bf16[4,2048]{1,0:T(4,128)(2,1)} %bitcast.18, ...), custom_call_target="tpu_custom_call" | custom-call | flops 2000000000 | bytes 8000000 | tf_op jit(solution)/shard_map/pallas_call | solution.py:458
  74.4 0.7 reshape.85
  75.1 0.0 copy-done
  75.1 0.7 bitcast_select_fusion
  75.8 1.4 %copy.19 = bf16[64,1,256]{2,0,1:T(8,128)(2,1)} copy(bf16[64,1,256]{2,0,1:T(8,128)(2,1)} %bitcast.14) | data formatting | bytes 65536
  (1 shorter events, 0.0 us)
Async XLA Ops:
  0.6 74.5 %copy-start = (s32[4,1]{0,1:T(1,128)S(1)}, s32[4,1]{0,1:T(1,128)}, u32[]{:S(2)}) copy-start(s32[4,1]{0,1:T(1,128)} %param.17) | copy-start | bytes 52

commit v3 on v2

--- a/solution.py
+++ b/solution.py
@@ -42,10 +42,10 @@
     tokens, w_in, w_group, w_out, w_step, taps_v, bias_v, group_taps_v, group_bias_v,
     step_bias_v, decay_v, skip_v, gain_v, load_sem,
     packed_taps, a_src, a_dst, b_src, b_dst, maps, x_src, x_dst, z_src, z_dst,
-    mixed, weights, gat, wide, sq_src, sq_dst, unscaled,
-    d1_src, d1_dst, own, d2_src, d2_dst, d3_src, d3_dst,
-    a_send, a_recv, b_send, b_recv, c_send, c_recv, x_send, x_recv, z_send, z_recv,
-    g_send, g_recv, q_send, q_recv, d1_send, d1_recv, d2_send, d2_recv, d3_send, d3_recv,
+    w_src, w_all, mixed, weights, gat, gathered, sq_src, sq_dst,
+    product, e_src, e_dst, d3_src, d3_dst,
+    a_send, a_recv, b_send, b_recv, c_send, c_recv, x_send, x_recv, z_send, z_recv, w_send, w_recv,
+    g_send, g_recv, f_send, f_recv, q_send, q_recv, e_send, e_recv, d3_send, d3_recv,
 ):
     rep = lax.axis_index("rep")
     samp = lax.axis_index("samp")
@@ -60,25 +60,6 @@
     def device(samp_index, tp_index):
         return (rep, samp_index, tp_index)
 
-    barrier = pltpu.get_barrier_semaphore()
-
-    def greet(samp_index, tp_index):
-        pl.semaphore_signal(barrier, inc=1, device_id=device(samp_index, tp_index), device_id_type=MESH)
-
-    for d in (2, 1, 3):
-        greet((samp + d) % 4, tp)
-    for i in range(4):
-        @pl.when(jnp.logical_or(low != samp, i != low))
-        def _():
-            greet(low, i * 8 + place)
-    for i in range(8):
-        @pl.when(quarter * 8 + i != tp)
-        def _():
-            greet(samp, quarter * 8 + i)
-    for d in range(1, 4):
-        greet(samp, group * 4 + (quarter + d) % 4)
-        greet(samp, low * 8 + ((across + d) % 4) * 2 + core)
-
     pairs = (
         (group_ref, w_group), (prompt_ref, tokens.at[pl.ds(0, PROMPT)]), (fresh_ref, tokens.at[pl.ds(PROMPT, FRESH)]),
         (group_taps_ref, group_taps_v), (group_bias_ref, group_bias_v), (step_ref, w_step),
@@ -86,7 +67,29 @@
         (step_bias_ref, step_bias_v), (decay_ref, decay_v), (skip_ref, skip_v), (gain_ref, gain_v), (out_ref, w_out),
     )
     loads = [pltpu.make_async_copy(a, b, load_sem.at[i]) for i, (a, b) in enumerate(pairs)]
-    for load in loads:
+    for load in loads[:3]:
+        load.start()
+
+    barrier = pltpu.get_barrier_semaphore()
+
+    def greet(samp_index, tp_index):
+        pl.semaphore_signal(barrier, inc=1, device_id=device(samp_index, tp_index), device_id_type=MESH)
+
+    for d in (2, 1, 3):
+        greet((samp + d) % 4, tp)
+    for i in range(4):
+        @pl.when(jnp.logical_or(low != samp, i != low))
+        def _():
+            greet(low, i * 8 + place)
+    for i in range(8):
+        @pl.when(quarter * 8 + i != tp)
+        def _():
+            greet(samp, quarter * 8 + i)
+    for d in range(1, 4):
+        greet(samp, group * 4 + (quarter + d) % 4)
+        greet(samp, low * 8 + ((across + d) % 4) * 2 + core)
+
+    for load in loads[3:]:
         load.start()
     sends = []
 
@@ -184,9 +187,22 @@
     b_copies = start([
         copy(b_src, b_dst.at[d - 1], b_send.at[d - 1], b_recv.at[d - 1], (samp + d) % 4, tp) for d in (2, 1, 3)
     ])
-    for one in b_copies:
-        one.wait_send()
-    z_copies = start(to_heads(z_src, z_dst, z_send, z_recv))
+
+    for load in loads[13:]:
+        load.wait()
+    gain = jnp.transpose(jnp.broadcast_to(gain_v[...], (128, CHANNELS)))
+    for to in range(4):
+        for part in range(4):
+            columns = pl.ds(512 * to + 128 * part, 128)
+            w_src[to, :, pl.ds(128 * part, 128)] = (w_out[:, columns].astype(F32) * gain).astype(BF16)
+    w_all[pl.ds(across, 1)] = w_src[pl.ds(across, 1)]
+    w_copies = start([
+        copy(
+            w_src.at[(across + d) % 4], w_all.at[across], w_send.at[d - 1], w_recv.at[d - 1],
+            samp, low * 8 + ((across + d) % 4) * 2 + core,
+        )
+        for d in (2, 1, 3)
+    ])
 
     lane128 = iota((1, 128), 1)
 
@@ -213,6 +229,7 @@
     rate = jnp.exp(own_scalar(decay_v))
     for one in x_copies:
         one.wait_recv()
+    z_copies = start(to_heads(z_src, z_dst, z_send, z_recv))
     summed = x_src[samp].astype(F32)
     for d in range(3):
         summed = summed + x_dst[d].astype(F32)
@@ -316,105 +333,92 @@
 
     lane_c = iota((BLOCK, 128), 1)
     g_copies = []
+
+    def onward(c, k):
+        piece = (samp - k + 4) % 4
+        return [
+            copy(
+                gat.at[c, across, piece], gat.at[c, across, piece], f_send.at[c, k, d - 1], f_recv.at[c, k, d - 1],
+                samp, low * 8 + ((across + d) % 4) * 2 + core,
+            )
+            for d in (2, 1, 3)
+        ]
+
+    f_copies = [[], []]
     for c in range(2):
         gated = halves[c] * gate[128 * c:128 * c + 128]
         upper = jnp.concatenate([gated[:64], fresh[32 * c:32 * c + 16]], axis=0)
         lower = jnp.concatenate([gated[64:], fresh[32 * c + 16:32 * c + 32]], axis=0)
-        gat[c, samp] = jnp.where(lane_c < 64, pltpu.roll(upper, 64, 1), lower).astype(BF16)
+        gat[c, across, samp] = jnp.where(lane_c < 64, pltpu.roll(upper, 64, 1), lower).astype(BF16)
         g_copies.append(start([
-            copy(gat.at[c, samp], gat.at[c, samp], g_send.at[c, d - 1], g_recv.at[c, d - 1], (samp + d) % 4, tp)
+            copy(
+                gat.at[c, across, samp], gat.at[c, across, samp], g_send.at[c, d - 1], g_recv.at[c, d - 1],
+                (samp + d) % 4, tp,
+            )
             for d in (2, 1, 3)
         ]))
-
-    for load in loads[13:]:
-        load.wait()
-
-    def d1_copy(c, i):
-        return copy(
-            d1_src.at[c, i], d1_dst.at[c, i], d1_send.at[c, i], d1_recv.at[c, i],
-            samp, low * 8 + across * 2 + 1 - core,
-        )
-
-    def d2_copy(d, s):
-        return copy(
-            d2_src.at[d - 1, s], d2_dst.at[d - 1, s], d2_send.at[d - 1, s], d2_recv.at[d - 1, s],
-            samp, low * 8 + ((across + d) % 4) * 2 + core,
-        )
+        f_copies[c] += start(onward(c, 0))
+    for c in range(2):
+        for k, at in ((1, 1), (3, 2), (2, 0)):
+            g_copies[c][at].wait_recv()
+            f_copies[c] += start(onward(c, k))
+
+    partner = low * 8 + across * 2 + 1 - core
+    sq_lane = iota((2 * BLOCK, 128), 1)
+    for one in w_copies:
+        one.wait_recv()
+    e_copies = []
+    for c in range(2):
+        for one in f_copies[c]:
+            one.wait_recv()
+        squares = []
+        for half in range(2):
+            total = jnp.zeros((2 * BLOCK, 128), F32)
+            for at in (2 * half, 2 * half + 1):
+                for pair in range(2):
+                    first, second = gat[c, at, 2 * pair].astype(F32), gat[c, at, 2 * pair + 1].astype(F32)
+                    both = jnp.concatenate([
+                        jnp.where(lane_c < 64, first, pltpu.roll(second, 64, 1)),
+                        jnp.where(lane_c < 64, pltpu.roll(first, 64, 1), second),
+                    ], axis=0)
+                    gathered[:, pl.ds(256 * at + 128 * pair, 128)] = both.astype(BF16)
+                    total = total + both * both
+            squares.append(jnp.sum(total, axis=1, keepdims=True))
+        sq_src[c] = jnp.where(sq_lane < 64, squares[0], squares[1])
+        q_copies = start([copy(sq_src.at[c], sq_dst.at[c], q_send.at[c], q_recv.at[c], samp, partner)])
+        products = [
+            mm(gathered[:, pl.ds(512 * half, 512)], w_all[2 * half:2 * half + 2].reshape(512, 512)) for half in range(2)
+        ]
+        q_copies[0].wait_recv()
+        scale = lax.rsqrt((sq_src[c] + sq_dst[c]) * (1.0 / 1024.0) + 1e-5)
+        scaled = products[0] * scale[:, 0:1] + products[1] * scale[:, 64:65]
+        product[c, 0] = scaled[:, :256]
+        product[c, 1] = scaled[:, 256:]
+        e_src[c] = product[c, 1 - core].astype(BF16)
+        e_copies += start([copy(e_src.at[c], e_dst.at[c], e_send.at[c], e_recv.at[c], samp, partner)])
 
     def d3_copy(s):
         return copy(d3_src.at[s], d3_dst.at[low], d3_send.at[s], d3_recv.at[low], s, samp * 8 + place)
 
-    for c in range(2):
-        for one in g_copies[c]:
-            one.wait_recv()
-        for pair in range(2):
-            first, second = gat[c, 2 * pair].astype(F32), gat[c, 2 * pair + 1].astype(F32)
-            columns = pl.ds(128 * pair, 128)
-            wide[pl.ds(0, BLOCK), columns] = jnp.where(lane_c < 64, first, pltpu.roll(second, 64, 1))
-            wide[pl.ds(BLOCK, BLOCK), columns] = jnp.where(lane_c < 64, pltpu.roll(first, 64, 1), second)
-        gathered = wide[...]
-        unscaled[...] = (gathered * gain_v[...]).astype(BF16)
-
-        squares = jnp.sum(gathered * gathered, axis=1, keepdims=True)
-        squares = jnp.concatenate([squares, jnp.zeros((96, 1), F32)], axis=0)
-        squares = jnp.transpose(jnp.broadcast_to(squares, (256, 128)))[0:8]
-        sq_src[c] = squares
-        q_copies = start([
-            copy(
-                sq_src.at[c], sq_dst.at[c, d - 1], q_send.at[c, d - 1], q_recv.at[c, d - 1],
-                samp, group * 4 + (quarter + d) % 4,
-            )
-            for d in (3, 2, 1)
-        ])
-
-        d1_copies = [d1_copy(c, i) for i in range(4)]
-        for i in range(4):
-            columns = pl.ds(pl.multiple_of((2 * i + 1 - core) * 256, 256), 256)
-            d1_src[c, i] = mm(unscaled[...], w_out[:, columns]).astype(BF16)
-            start([d1_copies[i]])
-        for i in range(4):
-            columns = pl.ds(pl.multiple_of((2 * i + core) * 256, 256), 256)
-            own[i] = mm(unscaled[...], w_out[:, columns])
-        for one in q_copies:
-            one.wait_recv()
-        for d in range(3):
-            squares = squares + sq_dst[c, d]
-        scale = lax.rsqrt(squares * (1.0 / 1024.0) + 1e-5)
-        scale = jnp.transpose(jnp.broadcast_to(scale[0:1], (128, 256)))[:160]
-        scale = jnp.concatenate([scale, scale], axis=1)
-        for one in d1_copies:
-            one.wait_recv()
-        for half in range(2):
-            s = 2 * c + half
-            rows = pl.ds(BLOCK * half, BLOCK)
-            by = scale[BLOCK * half:BLOCK * half + BLOCK]
-            for d in (2, 1, 3):
-                to = (across + d) % 4
-                d2_src[d - 1, s] = ((own[to, rows, :] + d1_dst[c, to, rows, :].astype(F32)) * by).astype(BF16)
-                start([d2_copy(d, s)])
-            kept = (own[across, rows, :] + d1_dst[c, across, rows, :].astype(F32)) * by
-            if s == 0:
-                kept_all = [kept]
-            else:
-                kept_all.append(kept)
-
     def stays(s):
         return jnp.logical_and(samp == low, samp == s)
 
-    for s in range(4):
-        value = kept_all[s]
-        for d in range(1, 4):
-            d2_copy(d, s).wait_recv()
-            value = value + d2_dst[d - 1, s].astype(F32)
-        d3_src[s] = value.astype(BF16)
-
-        @pl.when(stays(s))
-        def _():
-            d3_dst[low] = d3_src[s]
-
-        @pl.when(jnp.logical_not(stays(s)))
-        def _():
-            d3_copy(s).start()
+    for c in range(2):
+        e_copies[c].wait_recv()
+        outer = jnp.logical_or(samp == 0, samp == 3)
+        far = jnp.where(outer, 1 - c, c)
+        for half in (far, 1 - far):
+            rows = pl.ds(pl.multiple_of(BLOCK * half, 16), BLOCK)
+            s = 2 * c + half
+            d3_src[s] = (product[c, core, rows, :] + e_dst[c, rows, :].astype(F32)).astype(BF16)
+
+            @pl.when(stays(s))
+            def _():
+                d3_dst[low] = d3_src[s]
+
+            @pl.when(jnp.logical_not(stays(s)))
+            def _():
+                d3_copy(s).start()
 
     for i in range(4):
         @pl.when(jnp.logical_or(low != samp, i != low))
@@ -423,16 +427,16 @@
     value = d3_dst[0].astype(F32)
     for i in range(1, 4):
         value = value + d3_dst[i].astype(F32)
-    prefill_ref[...] = value[:64].astype(BF16)
-    decode_ref[...] = value[64:].astype(BF16)
+    prefill_ref[...] = value[:64]
+    for step in range(4):
+        decode_ref[step] = value[64 + 4 * step:68 + 4 * step]
 
     for g in range(8):
         @pl.when(g * 4 + low != tp)
         def _():
             a_copy(g).wait_send()
     for one in sends:
-        if not any(one is other for other in b_copies):
-            one.wait_send()
+        one.wait_send()
     for s in range(4):
         @pl.when(jnp.logical_not(stays(s)))
         def _():
@@ -458,8 +462,8 @@
     prefill, decode = pl.pallas_call(
         kernel,
         out_shape=(
-            jax.ShapeDtypeStruct((64, CHANNELS), BF16),
-            jax.ShapeDtypeStruct((16, CHANNELS), BF16),
+            jax.ShapeDtypeStruct((64, CHANNELS), F32),
+            jax.ShapeDtypeStruct((4, 4, CHANNELS), F32),
         ),
         in_specs=[anywhere] * 14,
         out_specs=(vector, vector),
@@ -473,15 +477,14 @@
             room(4, 64, PADDED),
             room(4, 176, 128), room(3, 176, 128),
             room(4, 160, 128), room(3, 160, 128),
+            room(4, CHANNELS, 512), room(4, CHANNELS, 512),
             room(PADDED, 128), wide_room(576, 128),
-            room(2, 4, BLOCK, 128), wide_room(2 * BLOCK, CHANNELS),
-            wide_room(2, 8, 256), wide_room(2, 3, 8, 256),
-            room(2 * BLOCK, CHANNELS),
-            room(2, 4, 2 * BLOCK, CHANNELS), room(2, 4, 2 * BLOCK, CHANNELS), wide_room(4, 2 * BLOCK, CHANNELS),
-            room(3, 4, BLOCK, CHANNELS), room(3, 4, BLOCK, CHANNELS),
+            room(2, 4, 4, BLOCK, 128), room(2 * BLOCK, 1024),
+            wide_room(2, 2 * BLOCK, 128), wide_room(2, 2 * BLOCK, 128),
+            wide_room(2, 2, 2 * BLOCK, CHANNELS), room(2, 2 * BLOCK, CHANNELS), room(2, 2 * BLOCK, CHANNELS),
             room(4, BLOCK, CHANNELS), room(4, BLOCK, CHANNELS),
-            dma(8), dma(8), dma(3), dma(3), dma(3), dma(3), dma(3), dma(3), dma(3), dma(3),
-            dma(2, 3), dma(2, 3), dma(2, 3), dma(2, 3), dma(2, 4), dma(2, 4), dma(3, 4), dma(3, 4), dma(4), dma(4),
+            dma(8), dma(8), dma(3), dma(3), dma(3), dma(3), dma(3), dma(3), dma(3), dma(3), dma(3), dma(3),
+            dma(2, 3), dma(2, 3), dma(2, 4, 3), dma(2, 4, 3), dma(2), dma(2), dma(2), dma(2), dma(4), dma(4),
         ],
         compiler_params=pltpu.CompilerParams(
             collective_id=0, has_side_effects=True, vmem_limit_bytes=VMEM_LIMIT
@@ -504,8 +507,8 @@
         norm_gain.reshape(1, CHANNELS),
     )
     active = jnp.arange(4)[:, None, None] < lengths[None]
-    decode = decode.reshape(4, 4, 1, CHANNELS)
-    return prefill.reshape(64, 1, CHANNELS), jnp.where(active[..., None], decode, jnp.zeros_like(decode))
+    decode = jnp.where(active, decode, 0.0).astype(BF16)
+    return prefill.astype(BF16)[:, None, :], decode[:, :, None, :]
 
 
 def solution(mesh):

time: 77.6 us -> 75.4 us (0.972)
  Pallas kernels: 73.8 us -> 71.2 us
  other arithmetic: 0.69 us -> 2.86 us
  local copies, waits for them, and re-layouts: 2.09 us -> 0.01 us
    pallas_call x1, Pallas kernels: 73.8 us -> 71.2 us  [shards(): pl.pallas_call(kernel, out_shape=(jax.ShapeDtypeStruct((64, CHANNELS), F3...]
    broadcast_in_dim x0 -> x1, other arithmetic: none -> 1.46 us  [shards(): return (prefill.astype(BF16)[:, None, :], decode[:, :, None, :])]
    unnamed x0 -> x1, other arithmetic: none -> 1.39 us
    unnamed x3 -> x2, local copies, waits for them, and re-layouts: 1.38 us -> 0.01 us
where the time goes in v3:
time: 75.4 us; the launch traced here: 74.7 us
  Pallas kernels  71.2 us (94%)
  other arithmetic  2.86 us (4%)
    pallas_call x1, Pallas kernels, shards(): pl.pallas_call(kernel, out_shape=(jax.ShapeDtypeStruct((64, CHANNELS), F3...  71.2 us

profile of v3, /device:TPU:24, one launch (start us, length us, event | category | flops | bytes accessed | tf_op | source)
XLA Modules:
  0.0 74.7 jit_solution(5637071563365843379)
XLA Ops:
  0.6 0.0 copy-start
  0.6 71.2 %shard_map.158 = (f32[64,256]{1,0:T(8,128)}, f32[4,4,256]{2,1,0:T(4,128)}) custom-call(bf16[256,2048]{1,0:T(8,128)(2,1)} %bitcast.17, bf16[64,2048]{1,0:T(8,128)(2,1)} %bitcast.18, bf16[2,2048,256]{2,1,0:T(8,128)(2,1)} %in_ref.1, bf16[64,2048]{1,0:T(8,128)(2,1)} %bitcast.19, bf16[256,2048]{1,0:T(8,128)(2,1)} %out_ref.1, bf16[4,2048]{1,0:T(4,128)(2,1)} %bitcast.20, ...), custom_call_target="tpu_custom_call" | custom-call | flops 2000000000 | bytes 8000000 | tf_op jit(solution)/shard_map/pallas_call | solution.py:462
  71.8 1.5 %convert_bitcast_fusion = bf16[64,1,256]{2,0,1:T(8,128)(2,1)} fusion(f32[64,256]{1,0:T(8,128)} %get-tuple-element.4), kind=kLoop, calls=%fused_computation | loop fusion | flops 16384 | bytes 98304 | tf_op jit(solution)/shard_map/broadcast_in_dim | solution.py:511
  73.3 0.0 copy-done
  73.3 1.4 %fusion = bf16[4,4,1,256]{3,1,2,0:T(4,128)(2,1)} fusion(f32[4,4,256]{2,1,0:T(4,128)} %get-tuple-element.5, pred[4,4]{1,0:T(4,128)(4,1)S(1)} %iota_compare_fusion), kind=kLoop, calls=%fused_computation.2 | loop fusion | flops 4096 | bytes 24592
  (1 shorter events, 0.0 us)
Async XLA Ops:
  0.6 72.7 %copy-start = (s32[4,1]{0,1:T(1,128)S(1)}, s32[4,1]{0,1:T(1,128)}, u32[]{:S(2)}) copy-start(s32[4,1]{0,1:T(1,128)} %param.17) | copy-start | bytes 52

commit v4 on v3

--- a/solution.py
+++ b/solution.py
@@ -38,11 +38,11 @@
 def kernel(
     prompt_ref, fresh_ref, in_ref, group_ref, out_ref, step_ref, taps_ref, bias_ref,
     group_taps_ref, group_bias_ref, step_bias_ref, decay_ref, skip_ref, gain_ref,
-    prefill_ref, decode_ref,
+    rows_ref,
     tokens, w_in, w_group, w_out, w_step, taps_v, bias_v, group_taps_v, group_bias_v,
     step_bias_v, decay_v, skip_v, gain_v, load_sem,
     packed_taps, a_src, a_dst, b_src, b_dst, maps, x_src, x_dst, z_src, z_dst,
-    w_src, w_all, mixed, weights, gat, gathered, sq_src, sq_dst,
+    w_src, w_all, mixed, weights, gat, gathered, sq_all,
     product, e_src, e_dst, d3_src, d3_dst,
     a_send, a_recv, b_send, b_recv, c_send, c_recv, x_send, x_recv, z_send, z_recv, w_send, w_recv,
     g_send, g_recv, f_send, f_recv, q_send, q_recv, e_send, e_recv, d3_send, d3_recv,
@@ -88,6 +88,7 @@
     for d in range(1, 4):
         greet(samp, group * 4 + (quarter + d) % 4)
         greet(samp, low * 8 + ((across + d) % 4) * 2 + core)
+        greet(samp, low * 8 + ((across + d) % 4) * 2 + 1 - core)
 
     for load in loads[3:]:
         load.start()
@@ -127,7 +128,7 @@
     a_src[:, :, pl.ds(PROMPT, 128)] = tail.reshape(8, 8, 128).astype(BF16)
 
     pl.semaphore_wait(
-        barrier, 19 + jnp.where(quarter != low, 1, 0) + jnp.where(samp != low, 1, 0)
+        barrier, 22 + jnp.where(quarter != low, 1, 0) + jnp.where(samp != low, 1, 0)
     )
 
     def a_copy(g):
@@ -331,71 +332,76 @@
     gate = silu(unpacked(gate.astype(BF16).astype(F32)))
     fresh = mm(requarter, (fresh * gate[PROMPT:]).astype(BF16))
 
-    lane_c = iota((BLOCK, 128), 1)
-    g_copies = []
-
-    def onward(c, k):
+    blocks = []
+    for i in range(4):
+        half = halves[i // 2] * gate[128 * (i // 2):128 * (i // 2) + 128]
+        blocks += [half[64 * (i % 2):64 * (i % 2) + 64], fresh[16 * i:16 * i + 16]]
+    upper = jnp.concatenate(blocks[:4], axis=0)
+    lower = jnp.concatenate(blocks[4:], axis=0)
+    gat[across, samp] = jnp.where(lane_h < 64, pltpu.roll(upper, 64, 1), lower).astype(BF16)
+    g_copies = start([
+        copy(gat.at[across, samp], gat.at[across, samp], g_send.at[d - 1], g_recv.at[d - 1], (samp + d) % 4, tp)
+        for d in (2, 1, 3)
+    ])
+
+    def onward(k):
         piece = (samp - k + 4) % 4
-        return [
+        return start([
             copy(
-                gat.at[c, across, piece], gat.at[c, across, piece], f_send.at[c, k, d - 1], f_recv.at[c, k, d - 1],
+                gat.at[across, piece], gat.at[across, piece], f_send.at[k, d - 1], f_recv.at[k, d - 1],
                 samp, low * 8 + ((across + d) % 4) * 2 + core,
             )
             for d in (2, 1, 3)
-        ]
-
-    f_copies = [[], []]
-    for c in range(2):
-        gated = halves[c] * gate[128 * c:128 * c + 128]
-        upper = jnp.concatenate([gated[:64], fresh[32 * c:32 * c + 16]], axis=0)
-        lower = jnp.concatenate([gated[64:], fresh[32 * c + 16:32 * c + 32]], axis=0)
-        gat[c, across, samp] = jnp.where(lane_c < 64, pltpu.roll(upper, 64, 1), lower).astype(BF16)
-        g_copies.append(start([
-            copy(
-                gat.at[c, across, samp], gat.at[c, across, samp], g_send.at[c, d - 1], g_recv.at[c, d - 1],
-                (samp + d) % 4, tp,
-            )
-            for d in (2, 1, 3)
-        ]))
-        f_copies[c] += start(onward(c, 0))
-    for c in range(2):
-        for k, at in ((1, 1), (3, 2), (2, 0)):
-            g_copies[c][at].wait_recv()
-            f_copies[c] += start(onward(c, k))
-
-    partner = low * 8 + across * 2 + 1 - core
-    sq_lane = iota((2 * BLOCK, 128), 1)
-    for one in w_copies:
+        ])
+
+    f_copies = onward(0)
+    for k, at in ((1, 1), (3, 2), (2, 0)):
+        g_copies[at].wait_recv()
+        f_copies += onward(k)
+
+    def side_by_side(at, pair):
+        first, second = gat[at, 2 * pair].astype(F32), gat[at, 2 * pair + 1].astype(F32)
+        return jnp.concatenate([
+            jnp.where(lane_h < 64, first, pltpu.roll(second, 64, 1)),
+            jnp.where(lane_h < 64, pltpu.roll(first, 64, 1), second),
+        ], axis=0)
+
+    squares = [side_by_side(across, pair) for pair in range(2)]
+    squares = jnp.sum(squares[0] * squares[0] + squares[1] * squares[1], axis=1, keepdims=True)
+    squares = jnp.concatenate([squares, jnp.zeros((PADDED - ROWS, 1), F32)], axis=0)
+    sq_all[place] = jnp.transpose(jnp.broadcast_to(squares, (PADDED, 128)))[0:1]
+
+    def q_copy(i):
+        return copy(sq_all.at[place], sq_all.at[place], q_send.at[i], q_recv.at[place], samp, low * 8 + i)
+
+    for i in range(8):
+        @pl.when(place != i)
+        def _():
+            q_copy(i).start()
+
+    for one in w_copies + f_copies:
         one.wait_recv()
-    e_copies = []
-    for c in range(2):
-        for one in f_copies[c]:
-            one.wait_recv()
-        squares = []
-        for half in range(2):
-            total = jnp.zeros((2 * BLOCK, 128), F32)
-            for at in (2 * half, 2 * half + 1):
-                for pair in range(2):
-                    first, second = gat[c, at, 2 * pair].astype(F32), gat[c, at, 2 * pair + 1].astype(F32)
-                    both = jnp.concatenate([
-                        jnp.where(lane_c < 64, first, pltpu.roll(second, 64, 1)),
-                        jnp.where(lane_c < 64, pltpu.roll(first, 64, 1), second),
-                    ], axis=0)
-                    gathered[:, pl.ds(256 * at + 128 * pair, 128)] = both.astype(BF16)
-                    total = total + both * both
-            squares.append(jnp.sum(total, axis=1, keepdims=True))
-        sq_src[c] = jnp.where(sq_lane < 64, squares[0], squares[1])
-        q_copies = start([copy(sq_src.at[c], sq_dst.at[c], q_send.at[c], q_recv.at[c], samp, partner)])
-        products = [
-            mm(gathered[:, pl.ds(512 * half, 512)], w_all[2 * half:2 * half + 2].reshape(512, 512)) for half in range(2)
-        ]
-        q_copies[0].wait_recv()
-        scale = lax.rsqrt((sq_src[c] + sq_dst[c]) * (1.0 / 1024.0) + 1e-5)
-        scaled = products[0] * scale[:, 0:1] + products[1] * scale[:, 64:65]
-        product[c, 0] = scaled[:, :256]
-        product[c, 1] = scaled[:, 256:]
-        e_src[c] = product[c, 1 - core].astype(BF16)
-        e_copies += start([copy(e_src.at[c], e_dst.at[c], e_send.at[c], e_recv.at[c], samp, partner)])
+    for at in range(4):
+        for pair in range(2):
+            gathered[:, pl.ds(256 * at + 128 * pair, 128)] = side_by_side(at, pair).astype(BF16)
+    products = [
+        mm(gathered[:, pl.ds(512 * half, 512)], w_all[2 * half:2 * half + 2].reshape(512, 512)) for half in range(2)
+    ]
+    for i in range(8):
+        @pl.when(place != i)
+        def _():
+            pltpu.make_async_copy(sq_all.at[i], sq_all.at[i], q_recv.at[i]).wait()
+    scales = []
+    for half in range(2):
+        total = sq_all[4 * half] + sq_all[4 * half + 1] + sq_all[4 * half + 2] + sq_all[4 * half + 3]
+        scale = jnp.broadcast_to(lax.rsqrt(total * (1.0 / 1024.0) + 1e-5), (128, PADDED))
+        scale = jnp.transpose(scale)[:ROWS]
+        scales.append(jnp.concatenate([scale] * 4, axis=1))
+    scaled = products[0] * scales[0] + products[1] * scales[1]
+    product[0] = scaled[:, :256]
+    product[1] = scaled[:, 256:]
+    e_src[...] = product[1 - core].astype(BF16)
+    e_copy = start([copy(e_src, e_dst, e_send.at[0], e_recv.at[0], samp, low * 8 + across * 2 + 1 - core)])[0]
 
     def d3_copy(s):
         return copy(d3_src.at[s], d3_dst.at[low], d3_send.at[s], d3_recv.at[low], s, samp * 8 + place)
@@ -403,22 +409,19 @@
     def stays(s):
         return jnp.logical_and(samp == low, samp == s)
 
-    for c in range(2):
-        e_copies[c].wait_recv()
-        outer = jnp.logical_or(samp == 0, samp == 3)
-        far = jnp.where(outer, 1 - c, c)
-        for half in (far, 1 - far):
-            rows = pl.ds(pl.multiple_of(BLOCK * half, 16), BLOCK)
-            s = 2 * c + half
-            d3_src[s] = (product[c, core, rows, :] + e_dst[c, rows, :].astype(F32)).astype(BF16)
-
-            @pl.when(stays(s))
-            def _():
-                d3_dst[low] = d3_src[s]
-
-            @pl.when(jnp.logical_not(stays(s)))
-            def _():
-                d3_copy(s).start()
+    e_copy.wait_recv()
+    for d in (2, 1, 3, 0):
+        s = (samp + d) % 4
+        rows = pl.ds(pl.multiple_of(BLOCK * s, 16), BLOCK)
+        d3_src[s] = (product[core, rows, :] + e_dst[rows, :].astype(F32)).astype(BF16)
+
+        @pl.when(stays(s))
+        def _():
+            d3_dst[low] = d3_src[s]
+
+        @pl.when(jnp.logical_not(stays(s)))
+        def _():
+            d3_copy(s).start()
 
     for i in range(4):
         @pl.when(jnp.logical_or(low != samp, i != low))
@@ -427,10 +430,12 @@
     value = d3_dst[0].astype(F32)
     for i in range(1, 4):
         value = value + d3_dst[i].astype(F32)
-    prefill_ref[...] = value[:64]
-    for step in range(4):
-        decode_ref[step] = value[64 + 4 * step:68 + 4 * step]
-
+    rows_ref[...] = value.astype(BF16)
+
+    for i in range(8):
+        @pl.when(place != i)
+        def _():
+            q_copy(i).wait_send()
     for g in range(8):
         @pl.when(g * 4 + low != tp)
         def _():
@@ -441,6 +446,17 @@
         @pl.when(jnp.logical_not(stays(s)))
         def _():
             d3_copy(s).wait_send()
+
+
+def finish(rows_ref, lengths_ref, prefill_ref, decode_ref):
+    prefill_ref[...] = rows_ref[:64]
+    step = iota((16, CHANNELS), 0)
+    lengths = jnp.zeros((16, CHANNELS), jnp.int32)
+    for i in range(4):
+        lengths = jnp.where(step % 4 == i, lengths_ref[0, i], lengths)
+    decode = jnp.where(step // 4 < lengths, rows_ref[64:].astype(F32), 0.0).astype(BF16)
+    for i in range(4):
+        decode_ref[i] = decode[4 * i:4 * i + 4]
 
 
 def shards(
@@ -459,14 +475,11 @@
     def wide_room(*shape):
         return pltpu.VMEM(shape, F32)
 
-    prefill, decode = pl.pallas_call(
+    rows = pl.pallas_call(
         kernel,
-        out_shape=(
-            jax.ShapeDtypeStruct((64, CHANNELS), F32),
-            jax.ShapeDtypeStruct((4, 4, CHANNELS), F32),
-        ),
+        out_shape=jax.ShapeDtypeStruct((BLOCK, CHANNELS), BF16),
         in_specs=[anywhere] * 14,
-        out_specs=(vector, vector),
+        out_specs=vector,
         scratch_shapes=[
             room(PADDED, WIDTH), room(2, WIDTH, CHANNELS), room(64, WIDTH), room(CHANNELS, WIDTH), room(4, WIDTH),
             wide_room(4, CHANNELS), wide_room(1, CHANNELS), wide_room(4, 64), wide_room(1, 64),
@@ -479,12 +492,11 @@
             room(4, 160, 128), room(3, 160, 128),
             room(4, CHANNELS, 512), room(4, CHANNELS, 512),
             room(PADDED, 128), wide_room(576, 128),
-            room(2, 4, 4, BLOCK, 128), room(2 * BLOCK, 1024),
-            wide_room(2, 2 * BLOCK, 128), wide_room(2, 2 * BLOCK, 128),
-            wide_room(2, 2, 2 * BLOCK, CHANNELS), room(2, 2 * BLOCK, CHANNELS), room(2, 2 * BLOCK, CHANNELS),
+            room(4, 4, 160, 128), room(ROWS, 1024), wide_room(8, 1, PADDED),
+            wide_room(2, ROWS, CHANNELS), room(ROWS, CHANNELS), room(ROWS, CHANNELS),
             room(4, BLOCK, CHANNELS), room(4, BLOCK, CHANNELS),
             dma(8), dma(8), dma(3), dma(3), dma(3), dma(3), dma(3), dma(3), dma(3), dma(3), dma(3), dma(3),
-            dma(2, 3), dma(2, 3), dma(2, 4, 3), dma(2, 4, 3), dma(2), dma(2), dma(2), dma(2), dma(4), dma(4),
+            dma(3), dma(3), dma(4, 3), dma(4, 3), dma(8), dma(8), dma(1), dma(1), dma(4), dma(4),
         ],
         compiler_params=pltpu.CompilerParams(
             collective_id=0, has_side_effects=True, vmem_limit_bytes=VMEM_LIMIT
@@ -506,9 +518,16 @@
         skip_gain.reshape(1, 4),
         norm_gain.reshape(1, CHANNELS),
     )
-    active = jnp.arange(4)[:, None, None] < lengths[None]
-    decode = jnp.where(active, decode, 0.0).astype(BF16)
-    return prefill.astype(BF16)[:, None, :], decode[:, :, None, :]
+    prefill, decode = pl.pallas_call(
+        finish,
+        out_shape=(
+            jax.ShapeDtypeStruct((64, CHANNELS), BF16),
+            jax.ShapeDtypeStruct((4, 4, CHANNELS), BF16),
+        ),
+        in_specs=[vector, pl.BlockSpec(memory_space=pltpu.SMEM)],
+        out_specs=(vector, vector),
+    )(rows, lengths.reshape(1, 4))
+    return prefill[:, None, :], decode[:, :, None, :]
 
 
 def solution(mesh):

time: 75.4 us -> 75.9 us (level)
  Pallas kernels: 71.2 us -> 74.3 us
  other arithmetic: 2.86 us -> 0 us
    pallas_call x1 -> x2, Pallas kernels: 71.2 us -> 74.3 us  [the longest x1 72.9 us: shards(): pl.pallas_call(kernel, out_shape=jax.ShapeDtypeStruct((BLOCK, CHANNELS),...]
    broadcast_in_dim x1 -> x0, other arithmetic: 1.46 us -> none  [shards(): return (prefill.astype(BF16)[:, None, :], decode[:, :, None, :])]
    unnamed x1 -> x0, other arithmetic: 1.39 us -> none
where the time goes in v4:
time: 75.9 us; the launch traced here: 75 us
  Pallas kernels  74.3 us (98%)
    pallas_call x1, Pallas kernels, shards(): pl.pallas_call(kernel, out_shape=jax.ShapeDtypeStruct((BLOCK, CHANNELS),...  72.9 us

profile of v4, /device:TPU:24, one launch (start us, length us, event | category | flops | bytes accessed | tf_op | source)
XLA Modules:
  0.0 75.0 jit_solution(4750404721147388222)
XLA Ops:
  0.6 72.9 %shard_map.158.rows_ref = bf16[80,256]{1,0:T(8,128)(2,1)} custom-call(bf16[256,2048]{1,0:T(8,128)(2,1)} %bitcast.16, bf16[64,2048]{1,0:T(8,128)(2,1)} %bitcast.17, bf16[2,2048,256]{2,1,0:T(8,128)(2,1)} %in_ref.1, bf16[64,2048]{1,0:T(8,128)(2,1)} %bitcast.18, bf16[256,2048]{1,0:T(8,128)(2,1)} %out_ref.1, bf16[4,2048]{1,0:T(4,128)(2,1)} %bitcast.20, ...), custom_call_target="tpu_custom_call" | custom-call | flops 2000000000 | bytes 8000000 | tf_op jit(solution)/shard_map/pallas_call | solution.py:478
  73.5 1.4 %shard_map.159 = (bf16[64,256]{1,0:T(8,128)(2,1)}, bf16[4,4,256]{2,1,0:T(4,128)(2,1)}) custom-call(bf16[80,256]{1,0:T(8,128)(2,1)} %shard_map.158.rows_ref, s32[1,4]{1,0:T(1,128)} %bitcast.15), custom_call_target="tpu_custom_call" | custom-call | tf_op jit(solution)/shard_map/pallas_call | solution.py:521

commit v5 on v4

--- a/solution.py
+++ b/solution.py
@@ -41,7 +41,7 @@
     rows_ref,
     tokens, w_in, w_group, w_out, w_step, taps_v, bias_v, group_taps_v, group_bias_v,
     step_bias_v, decay_v, skip_v, gain_v, load_sem,
-    packed_taps, a_src, a_dst, b_src, b_dst, maps, x_src, x_dst, z_src, z_dst,
+    packed_taps, a_src, a_dst, b_src, b_mid, b_in, maps, x_src, x_by, x_on, x_in, z_src, z_by, z_on, z_in,
     w_src, w_all, mixed, weights, gat, gathered, sq_all,
     product, e_src, e_dst, d3_src, d3_dst,
     a_send, a_recv, b_send, b_recv, c_send, c_recv, x_send, x_recv, z_send, z_recv, w_send, w_recv,
@@ -152,11 +152,25 @@
             return jnp.where(lane_h < 64, upper, pltpu.roll(lower, 64, 1)).astype(BF16)
         return jnp.where(lane_h < 64, pltpu.roll(upper, 64, 1), lower).astype(BF16)
 
-    def to_heads(source, target, send, recv):
-        return [
-            copy(source.at[(samp + d) % 4], target.at[d - 1], send.at[d - 1], recv.at[d - 1], (samp + d) % 4, tp)
-            for d in (2, 1, 3)
-        ]
+    above, below, opposite = (samp + 1) % 4, (samp + 3) % 4, (samp + 2) % 4
+
+    def first_leg(source, by, into, send, recv):
+        top, rest = pl.ds(0, BLOCK), pl.ds(BLOCK, source.shape[1] - BLOCK)
+        return start([
+            copy(source.at[opposite, top], by.at[top], send.at[0], recv.at[0], above, tp),
+            copy(source.at[opposite, rest], by.at[rest], send.at[1], recv.at[1], below, tp),
+            copy(source.at[above, rest], into.at[0, rest], send.at[2], recv.at[2], above, tp),
+            copy(source.at[below, top], into.at[1, top], send.at[3], recv.at[3], below, tp),
+        ])
+
+    def second_leg(first, source, by, on, into, send, recv):
+        top, rest = pl.ds(0, BLOCK), pl.ds(BLOCK, source.shape[1] - BLOCK)
+        copies = []
+        for i, (rows, to) in enumerate(((top, above), (rest, below))):
+            first[i].wait_recv()
+            on[rows, :] = (source[to, rows, :].astype(F32) + by[rows, :].astype(F32)).astype(BF16)
+            copies += start([copy(on.at[rows], into.at[i, rows], send.at[4 + i], recv.at[4 + i], to, tp)])
+        return first[2:] + copies
 
     loads[5].wait()
     sizes = mm_nt(w_step[...], tokens[...])
@@ -169,7 +183,7 @@
         for b in range(3):
             piece = jnp.where(size_row == b, sizes[h:h + 1, 128 * b:128 * b + 128], piece)
         x_src[h, pl.ds(160, 16), :] = piece.astype(BF16)
-    x_copies = start(to_heads(x_src, x_dst, x_send, x_recv))
+    x_copies = first_leg(x_src, x_by, x_in, x_send, x_recv)
     loads[7].wait()
     gate_part = mm(tokens[pl.ds(0, ROWS), :], w_in[0])
     for h in range(4):
@@ -185,9 +199,24 @@
     b_src[pl.ds(0, 64), :] = own_maps[:, 0:128].astype(BF16)
     b_src[pl.ds(64, 64), :] = own_maps[:, 128:256].astype(BF16)
     b_src[pl.ds(128, 32), :] = jnp.where(lane_q < 64, fresh_maps[:32], pltpu.roll(fresh_maps[32:], 64, 1)).astype(BF16)
-    b_copies = start([
-        copy(b_src, b_dst.at[d - 1], b_send.at[d - 1], b_recv.at[d - 1], (samp + d) % 4, tp) for d in (2, 1, 3)
-    ])
+    pairings = (samp + 1 - 2 * (samp % 2), 3 - samp)
+    b_rows = (pl.ds(0, BLOCK), pl.ds(BLOCK, BLOCK))
+
+    def b_step(step, source):
+        copies = []
+        for i, rows in enumerate(b_rows):
+            if step == 1:
+                b_copies[i].wait_recv()
+                b_mid[rows, :] = (b_src[rows, :].astype(F32) + b_in[0, rows, :].astype(F32)).astype(BF16)
+            copies += start([
+                copy(
+                    source.at[rows], b_in.at[step, rows], b_send.at[step, i], b_recv.at[step, i],
+                    pairings[(i + step) % 2], tp,
+                )
+            ])
+        return copies
+
+    b_copies = b_step(0, b_src)
 
     for load in loads[13:]:
         load.wait()
@@ -205,6 +234,10 @@
         for d in (2, 1, 3)
     ])
 
+    x_copies = second_leg(x_copies, x_src, x_by, x_on, x_in, x_send, x_recv)
+    b_copies = b_step(1, b_mid)
+    z_copies = first_leg(z_src, z_by, z_in, z_send, z_recv)
+
     lane128 = iota((1, 128), 1)
 
     def of_head(value):
@@ -228,12 +261,10 @@
     skip = own_scalar(skip_v)
     step_bias = own_scalar(step_bias_v)
     rate = jnp.exp(own_scalar(decay_v))
+    z_copies = second_leg(z_copies, z_src, z_by, z_on, z_in, z_send, z_recv)
     for one in x_copies:
         one.wait_recv()
-    z_copies = start(to_heads(z_src, z_dst, z_send, z_recv))
-    summed = x_src[samp].astype(F32)
-    for d in range(3):
-        summed = summed + x_dst[d].astype(F32)
+    summed = x_src[samp].astype(F32) + x_in[0].astype(F32) + x_in[1].astype(F32)
     summed = summed.astype(BF16).astype(F32)
     heads = unpacked(summed[:160])
     before = heads[:PROMPT]
@@ -280,9 +311,7 @@
 
     for one in b_copies:
         one.wait_recv()
-    total = b_src[...].astype(F32)
-    for d in range(3):
-        total = total + b_dst[d].astype(F32)
+    total = b_mid[...].astype(F32) + b_in[1].astype(F32)
     total = total.astype(BF16).astype(F32)
     taps = [own_maps[:, 320 + k:321 + k] + own_maps[:, 328 + k:329 + k] for k in range(5)]
     before = jnp.concatenate([total[0:64], total[64:128]], axis=1)
@@ -326,49 +355,54 @@
     halves = [read(0, 128, ((0, 192),)), read(128, 128, ((0, 320), (1, 448)))]
     for one in z_copies:
         one.wait_recv()
-    gate = z_src[samp].astype(F32)
-    for d in range(3):
-        gate = gate + z_dst[d].astype(F32)
+    gate = z_src[samp].astype(F32) + z_in[0].astype(F32) + z_in[1].astype(F32)
     gate = silu(unpacked(gate.astype(BF16).astype(F32)))
     fresh = mm(requarter, (fresh * gate[PROMPT:]).astype(BF16))
 
-    blocks = []
-    for i in range(4):
-        half = halves[i // 2] * gate[128 * (i // 2):128 * (i // 2) + 128]
-        blocks += [half[64 * (i % 2):64 * (i % 2) + 64], fresh[16 * i:16 * i + 16]]
-    upper = jnp.concatenate(blocks[:4], axis=0)
-    lower = jnp.concatenate(blocks[4:], axis=0)
-    gat[across, samp] = jnp.where(lane_h < 64, pltpu.roll(upper, 64, 1), lower).astype(BF16)
-    g_copies = start([
-        copy(gat.at[across, samp], gat.at[across, samp], g_send.at[d - 1], g_recv.at[d - 1], (samp + d) % 4, tp)
-        for d in (2, 1, 3)
-    ])
-
-    def onward(k):
+    lane_c = iota((BLOCK, 128), 1)
+
+    def onward(c, k):
         piece = (samp - k + 4) % 4
         return start([
             copy(
-                gat.at[across, piece], gat.at[across, piece], f_send.at[k, d - 1], f_recv.at[k, d - 1],
+                gat.at[c, across, piece], gat.at[c, across, piece], f_send.at[c, k, d - 1], f_recv.at[c, k, d - 1],
                 samp, low * 8 + ((across + d) % 4) * 2 + core,
             )
             for d in (2, 1, 3)
         ])
 
-    f_copies = onward(0)
-    for k, at in ((1, 1), (3, 2), (2, 0)):
-        g_copies[at].wait_recv()
-        f_copies += onward(k)
-
-    def side_by_side(at, pair):
-        first, second = gat[at, 2 * pair].astype(F32), gat[at, 2 * pair + 1].astype(F32)
+    for c in range(2):
+        gated = halves[c] * gate[128 * c:128 * c + 128]
+        upper = jnp.concatenate([gated[:64], fresh[32 * c:32 * c + 16]], axis=0)
+        lower = jnp.concatenate([gated[64:], fresh[32 * c + 16:32 * c + 32]], axis=0)
+        gat[c, across, samp] = jnp.where(lane_c < 64, pltpu.roll(upper, 64, 1), lower).astype(BF16)
+    g_copies = [{}, {}]
+    for d in (2, 1, 3):
+        for c in range(2):
+            g_copies[c][d] = start([
+                copy(
+                    gat.at[c, across, samp], gat.at[c, across, samp], g_send.at[c, d - 1], g_recv.at[c, d - 1],
+                    (samp + d) % 4, tp,
+                )
+            ])[0]
+    f_copies = [onward(c, 0) for c in range(2)]
+    for k in (1, 3, 2):
+        for c in range(2):
+            g_copies[c][k].wait_recv()
+            f_copies[c] += onward(c, k)
+
+    def side_by_side(c, at, pair):
+        first, second = gat[c, at, 2 * pair].astype(F32), gat[c, at, 2 * pair + 1].astype(F32)
         return jnp.concatenate([
-            jnp.where(lane_h < 64, first, pltpu.roll(second, 64, 1)),
-            jnp.where(lane_h < 64, pltpu.roll(first, 64, 1), second),
+            jnp.where(lane_c < 64, first, pltpu.roll(second, 64, 1)),
+            jnp.where(lane_c < 64, pltpu.roll(first, 64, 1), second),
         ], axis=0)
 
-    squares = [side_by_side(across, pair) for pair in range(2)]
-    squares = jnp.sum(squares[0] * squares[0] + squares[1] * squares[1], axis=1, keepdims=True)
-    squares = jnp.concatenate([squares, jnp.zeros((PADDED - ROWS, 1), F32)], axis=0)
+    squares = []
+    for c in range(2):
+        parts = [side_by_side(c, across, pair) for pair in range(2)]
+        squares.append(jnp.sum(parts[0] * parts[0] + parts[1] * parts[1], axis=1, keepdims=True))
+    squares = jnp.concatenate(squares + [jnp.zeros((PADDED - ROWS, 1), F32)], axis=0)
     sq_all[place] = jnp.transpose(jnp.broadcast_to(squares, (PADDED, 128)))[0:1]
 
     def q_copy(i):
@@ -379,29 +413,39 @@
         def _():
             q_copy(i).start()
 
-    for one in w_copies + f_copies:
+    for one in w_copies:
         one.wait_recv()
-    for at in range(4):
-        for pair in range(2):
-            gathered[:, pl.ds(256 * at + 128 * pair, 128)] = side_by_side(at, pair).astype(BF16)
-    products = [
-        mm(gathered[:, pl.ds(512 * half, 512)], w_all[2 * half:2 * half + 2].reshape(512, 512)) for half in range(2)
-    ]
-    for i in range(8):
-        @pl.when(place != i)
-        def _():
-            pltpu.make_async_copy(sq_all.at[i], sq_all.at[i], q_recv.at[i]).wait()
-    scales = []
-    for half in range(2):
-        total = sq_all[4 * half] + sq_all[4 * half + 1] + sq_all[4 * half + 2] + sq_all[4 * half + 3]
-        scale = jnp.broadcast_to(lax.rsqrt(total * (1.0 / 1024.0) + 1e-5), (128, PADDED))
-        scale = jnp.transpose(scale)[:ROWS]
-        scales.append(jnp.concatenate([scale] * 4, axis=1))
-    scaled = products[0] * scales[0] + products[1] * scales[1]
-    product[0] = scaled[:, :256]
-    product[1] = scaled[:, 256:]
-    e_src[...] = product[1 - core].astype(BF16)
-    e_copy = start([copy(e_src, e_dst, e_send.at[0], e_recv.at[0], samp, low * 8 + across * 2 + 1 - core)])[0]
+    e_copies = []
+    for c in range(2):
+        for one in f_copies[c]:
+            one.wait_recv()
+        for at in range(4):
+            for pair in range(2):
+                gathered[:, pl.ds(256 * at + 128 * pair, 128)] = side_by_side(c, at, pair).astype(BF16)
+        products = [
+            mm(gathered[:, pl.ds(512 * half, 512)], w_all[2 * half:2 * half + 2].reshape(512, 512)) for half in range(2)
+        ]
+        if c == 0:
+            for i in range(8):
+                @pl.when(place != i)
+                def _():
+                    pltpu.make_async_copy(sq_all.at[i], sq_all.at[i], q_recv.at[i]).wait()
+            scales = []
+            for half in range(2):
+                total = sq_all[4 * half] + sq_all[4 * half + 1] + sq_all[4 * half + 2] + sq_all[4 * half + 3]
+                scale = jnp.broadcast_to(lax.rsqrt(total * (1.0 / 1024.0) + 1e-5), (128, PADDED))
+                scales.append(jnp.transpose(scale))
+        scaled = [
+            products[half] * jnp.concatenate([scales[half][2 * BLOCK * c:2 * BLOCK * c + 2 * BLOCK]] * 4, axis=1)
+            for half in range(2)
+        ]
+        scaled = scaled[0] + scaled[1]
+        product[c, 0] = scaled[:, :256]
+        product[c, 1] = scaled[:, 256:]
+        e_src[c] = product[c, 1 - core].astype(BF16)
+        e_copies += start([
+            copy(e_src.at[c], e_dst.at[c], e_send.at[c], e_recv.at[c], samp, low * 8 + across * 2 + 1 - core)
+        ])
 
     def d3_copy(s):
         return copy(d3_src.at[s], d3_dst.at[low], d3_send.at[s], d3_recv.at[low], s, samp * 8 + place)
@@ -409,19 +453,22 @@
     def stays(s):
         return jnp.logical_and(samp == low, samp == s)
 
-    e_copy.wait_recv()
-    for d in (2, 1, 3, 0):
-        s = (samp + d) % 4
-        rows = pl.ds(pl.multiple_of(BLOCK * s, 16), BLOCK)
-        d3_src[s] = (product[core, rows, :] + e_dst[rows, :].astype(F32)).astype(BF16)
-
-        @pl.when(stays(s))
-        def _():
-            d3_dst[low] = d3_src[s]
-
-        @pl.when(jnp.logical_not(stays(s)))
-        def _():
-            d3_copy(s).start()
+    for c in range(2):
+        e_copies[c].wait_recv()
+        outer = jnp.logical_or(samp == 0, samp == 3)
+        far = jnp.where(outer, 1 - c, c)
+        for half in (far, 1 - far):
+            rows = pl.ds(pl.multiple_of(BLOCK * half, 16), BLOCK)
+            s = 2 * c + half
+            d3_src[s] = (product[c, core, rows, :] + e_dst[c, rows, :].astype(F32)).astype(BF16)
+
+            @pl.when(stays(s))
+            def _():
+                d3_dst[low] = d3_src[s]
+
+            @pl.when(jnp.logical_not(stays(s)))
+            def _():
+                d3_copy(s).start()
 
     for i in range(4):
         @pl.when(jnp.logical_or(low != samp, i != low))
@@ -486,17 +533,17 @@
             wide_room(1, 4), wide_room(1, 4), wide_room(1, 4), wide_room(1, CHANNELS), dma(15),
             wide_room(128, 64),
             room(8, 8, PADDED), room(8, 8, PADDED),
-            room(160, 128), room(3, 160, 128),
+            room(160, 128), room(160, 128), room(2, 160, 128),
             room(4, 64, PADDED),
-            room(4, 176, 128), room(3, 176, 128),
-            room(4, 160, 128), room(3, 160, 128),
+            room(4, 176, 128), room(176, 128), room(176, 128), room(2, 176, 128),
+            room(4, 160, 128), room(160, 128), room(160, 128), room(2, 160, 128),
             room(4, CHANNELS, 512), room(4, CHANNELS, 512),
             room(PADDED, 128), wide_room(576, 128),
-            room(4, 4, 160, 128), room(ROWS, 1024), wide_room(8, 1, PADDED),
-            wide_room(2, ROWS, CHANNELS), room(ROWS, CHANNELS), room(ROWS, CHANNELS),
+            room(2, 4, 4, BLOCK, 128), room(2 * BLOCK, 1024), wide_room(8, 1, PADDED),
+            wide_room(2, 2, 2 * BLOCK, CHANNELS), room(2, 2 * BLOCK, CHANNELS), room(2, 2 * BLOCK, CHANNELS),
             room(4, BLOCK, CHANNELS), room(4, BLOCK, CHANNELS),
-            dma(8), dma(8), dma(3), dma(3), dma(3), dma(3), dma(3), dma(3), dma(3), dma(3), dma(3), dma(3),
-            dma(3), dma(3), dma(4, 3), dma(4, 3), dma(8), dma(8), dma(1), dma(1), dma(4), dma(4),
+            dma(8), dma(8), dma(2, 2), dma(2, 2), dma(3), dma(3), dma(6), dma(6), dma(6), dma(6), dma(3), dma(3),
+            dma(2, 3), dma(2, 3), dma(2, 4, 3), dma(2, 4, 3), dma(8), dma(8), dma(2), dma(2), dma(4), dma(4),
         ],
         compiler_params=pltpu.CompilerParams(
             collective_id=0, has_side_effects=True, vmem_limit_bytes=VMEM_LIMIT

time: 75.9 us -> 71.5 us (0.942)
  Pallas kernels: 74.3 us -> 69.6 us
    pallas_call x1, Pallas kernels: 72.9 us -> 68.2 us  [shards(): pl.pallas_call(kernel, out_shape=jax.ShapeDtypeStruct((BLOCK, CHANNELS),...]
where the time goes in v5:
time: 71.5 us; the launch traced here: 70.3 us
  Pallas kernels  69.6 us (97%)
    pallas_call x1, Pallas kernels, shards(): pl.pallas_call(kernel, out_shape=jax.ShapeDtypeStruct((BLOCK, CHANNELS),...  68.2 us

profile of v5, /device:TPU:24, one launch (start us, length us, event | category | flops | bytes accessed | tf_op | source)
XLA Modules:
  0.0 70.3 jit_solution(2763425832551015140)
XLA Ops:
  0.6 68.2 %shard_map.158.rows_ref = bf16[80,256]{1,0:T(8,128)(2,1)} custom-call(bf16[256,2048]{1,0:T(8,128)(2,1)} %bitcast.16, bf16[64,2048]{1,0:T(8,128)(2,1)} %bitcast.17, bf16[2,2048,256]{2,1,0:T(8,128)(2,1)} %in_ref.1, bf16[64,2048]{1,0:T(8,128)(2,1)} %bitcast.18, bf16[256,2048]{1,0:T(8,128)(2,1)} %out_ref.1, bf16[4,2048]{1,0:T(4,128)(2,1)} %bitcast.20, ...), custom_call_target="tpu_custom_call" | custom-call | flops 2000000000 | bytes 8000000 | tf_op jit(solution)/shard_map/pallas_call | solution.py:525
  68.8 1.4 %shard_map.159 = (bf16[64,256]{1,0:T(8,128)(2,1)}, bf16[4,4,256]{2,1,0:T(4,128)(2,1)}) custom-call(bf16[80,256]{1,0:T(8,128)(2,1)} %shard_map.158.rows_ref, s32[1,4]{1,0:T(1,128)} %bitcast.15), custom_call_target="tpu_custom_call" | custom-call | tf_op jit(solution)/shard_map/pallas_call | solution.py:568

commit v6 on v5

--- a/solution.py
+++ b/solution.py
@@ -184,40 +184,6 @@
             piece = jnp.where(size_row == b, sizes[h:h + 1, 128 * b:128 * b + 128], piece)
         x_src[h, pl.ds(160, 16), :] = piece.astype(BF16)
     x_copies = first_leg(x_src, x_by, x_in, x_send, x_recv)
-    loads[7].wait()
-    gate_part = mm(tokens[pl.ds(0, ROWS), :], w_in[0])
-    for h in range(4):
-        z_src[h] = packed(gate_part, h)
-
-    for i in range(8):
-        @pl.when(quarter * 8 + i != tp)
-        def _():
-            pltpu.make_async_copy(a_dst.at[i], a_dst.at[i], a_recv.at[i]).wait()
-    own_maps = a_dst[...].astype(F32).reshape(64, PADDED)
-    lane_q = iota((32, 128), 1)
-    fresh_maps = own_maps[:, PROMPT:]
-    b_src[pl.ds(0, 64), :] = own_maps[:, 0:128].astype(BF16)
-    b_src[pl.ds(64, 64), :] = own_maps[:, 128:256].astype(BF16)
-    b_src[pl.ds(128, 32), :] = jnp.where(lane_q < 64, fresh_maps[:32], pltpu.roll(fresh_maps[32:], 64, 1)).astype(BF16)
-    pairings = (samp + 1 - 2 * (samp % 2), 3 - samp)
-    b_rows = (pl.ds(0, BLOCK), pl.ds(BLOCK, BLOCK))
-
-    def b_step(step, source):
-        copies = []
-        for i, rows in enumerate(b_rows):
-            if step == 1:
-                b_copies[i].wait_recv()
-                b_mid[rows, :] = (b_src[rows, :].astype(F32) + b_in[0, rows, :].astype(F32)).astype(BF16)
-            copies += start([
-                copy(
-                    source.at[rows], b_in.at[step, rows], b_send.at[step, i], b_recv.at[step, i],
-                    pairings[(i + step) % 2], tp,
-                )
-            ])
-        return copies
-
-    b_copies = b_step(0, b_src)
-
     for load in loads[13:]:
         load.wait()
     gain = jnp.transpose(jnp.broadcast_to(gain_v[...], (128, CHANNELS)))
@@ -233,6 +199,40 @@
         )
         for d in (2, 1, 3)
     ])
+
+    loads[7].wait()
+    gate_part = mm(tokens[pl.ds(0, ROWS), :], w_in[0])
+    for h in range(4):
+        z_src[h] = packed(gate_part, h)
+
+    for i in range(8):
+        @pl.when(quarter * 8 + i != tp)
+        def _():
+            pltpu.make_async_copy(a_dst.at[i], a_dst.at[i], a_recv.at[i]).wait()
+    own_maps = a_dst[...].astype(F32).reshape(64, PADDED)
+    lane_q = iota((32, 128), 1)
+    fresh_maps = own_maps[:, PROMPT:]
+    b_src[pl.ds(0, 64), :] = own_maps[:, 0:128].astype(BF16)
+    b_src[pl.ds(64, 64), :] = own_maps[:, 128:256].astype(BF16)
+    b_src[pl.ds(128, 32), :] = jnp.where(lane_q < 64, fresh_maps[:32], pltpu.roll(fresh_maps[32:], 64, 1)).astype(BF16)
+    pairings = (samp + 1 - 2 * (samp % 2), 3 - samp)
+    b_rows = (pl.ds(0, BLOCK), pl.ds(BLOCK, BLOCK))
+
+    def b_step(step, source):
+        copies = []
+        for i, rows in enumerate(b_rows):
+            if step == 1:
+                b_copies[i].wait_recv()
+                b_mid[rows, :] = (b_src[rows, :].astype(F32) + b_in[0, rows, :].astype(F32)).astype(BF16)
+            copies += start([
+                copy(
+                    source.at[rows], b_in.at[step, rows], b_send.at[step, i], b_recv.at[step, i],
+                    pairings[(i + step) % 2], tp,
+                )
+            ])
+        return copies
+
+    b_copies = b_step(0, b_src)
 
     x_copies = second_leg(x_copies, x_src, x_by, x_on, x_in, x_send, x_recv)
     b_copies = b_step(1, b_mid)

time: 71.5 us -> 71.1 us (level)
  no operation moved by 1% of the time
where the time goes in v6:
time: 71.1 us; the launch traced here: 70.2 us
  Pallas kernels  69.5 us (98%)
    pallas_call x1, Pallas kernels, shards(): pl.pallas_call(kernel, out_shape=jax.ShapeDtypeStruct((BLOCK, CHANNELS),...  68.1 us

profile of v6, /device:TPU:24, one launch (start us, length us, event | category | flops | bytes accessed | tf_op | source)
XLA Modules:
  0.0 70.2 jit_solution(13848113371772266649)
XLA Ops:
  0.6 68.1 %shard_map.158.rows_ref = bf16[80,256]{1,0:T(8,128)(2,1)} custom-call(bf16[256,2048]{1,0:T(8,128)(2,1)} %bitcast.16, bf16[64,2048]{1,0:T(8,128)(2,1)} %bitcast.17, bf16[2,2048,256]{2,1,0:T(8,128)(2,1)} %in_ref.1, bf16[64,2048]{1,0:T(8,128)(2,1)} %bitcast.18, bf16[256,2048]{1,0:T(8,128)(2,1)} %out_ref.1, bf16[4,2048]{1,0:T(4,128)(2,1)} %bitcast.20, ...), custom_call_target="tpu_custom_call" | custom-call | flops 2000000000 | bytes 8000000 | tf_op jit(solution)/shard_map/pallas_call | solution.py:525
  68.7 1.4 %shard_map.159 = (bf16[64,256]{1,0:T(8,128)(2,1)}, bf16[4,4,256]{2,1,0:T(4,128)(2,1)}) custom-call(bf16[80,256]{1,0:T(8,128)(2,1)} %shard_map.158.rows_ref, s32[1,4]{1,0:T(1,128)} %bitcast.15), custom_call_target="tpu_custom_call" | custom-call | tf_op jit(solution)/shard_map/pallas_call | solution.py:568

commit v7 on v6

--- a/solution.py
+++ b/solution.py
@@ -154,14 +154,14 @@
 
     above, below, opposite = (samp + 1) % 4, (samp + 3) % 4, (samp + 2) % 4
 
-    def first_leg(source, by, into, send, recv):
+    def first_leg(source, by, into, send, recv, part=slice(4)):
         top, rest = pl.ds(0, BLOCK), pl.ds(BLOCK, source.shape[1] - BLOCK)
         return start([
             copy(source.at[opposite, top], by.at[top], send.at[0], recv.at[0], above, tp),
             copy(source.at[opposite, rest], by.at[rest], send.at[1], recv.at[1], below, tp),
             copy(source.at[above, rest], into.at[0, rest], send.at[2], recv.at[2], above, tp),
             copy(source.at[below, top], into.at[1, top], send.at[3], recv.at[3], below, tp),
-        ])
+        ][part])
 
     def second_leg(first, source, by, on, into, send, recv):
         top, rest = pl.ds(0, BLOCK), pl.ds(BLOCK, source.shape[1] - BLOCK)
@@ -205,6 +205,8 @@
     for h in range(4):
         z_src[h] = packed(gate_part, h)
 
+    z_copies = first_leg(z_src, z_by, z_in, z_send, z_recv, slice(2))
+
     for i in range(8):
         @pl.when(quarter * 8 + i != tp)
         def _():
@@ -236,7 +238,6 @@
 
     x_copies = second_leg(x_copies, x_src, x_by, x_on, x_in, x_send, x_recv)
     b_copies = b_step(1, b_mid)
-    z_copies = first_leg(z_src, z_by, z_in, z_send, z_recv)
 
     lane128 = iota((1, 128), 1)
 
@@ -261,6 +262,7 @@
     skip = own_scalar(skip_v)
     step_bias = own_scalar(step_bias_v)
     rate = jnp.exp(own_scalar(decay_v))
+    z_copies += first_leg(z_src, z_by, z_in, z_send, z_recv, slice(2, 4))
     z_copies = second_leg(z_copies, z_src, z_by, z_on, z_in, z_send, z_recv)
     for one in x_copies:
         one.wait_recv()

time: 71.1 us -> 70.5 us (level)
  the two profiles are of different devices: /device:TPU:24 before, /device:TPU:121 now
where the time goes in v7:
time: 70.5 us; the launch traced here: 70.3 us
  Pallas kernels  69.6 us (99%)
    pallas_call x1, Pallas kernels, shards(): pl.pallas_call(kernel, out_shape=jax.ShapeDtypeStruct((BLOCK, CHANNELS),...  68.2 us
    pallas_call x1, Pallas kernels, shards(): pl.pallas_call(finish, out_shape=(jax.ShapeDtypeStruct((64, CHANNELS), BF...  1.42 us

profile of v7, /device:TPU:121, one launch (start us, length us, event | category | flops | bytes accessed | tf_op | source)
XLA Modules:
  0.0 70.3 jit_solution(6831551622482359969)
XLA Ops:
  0.6 68.2 %shard_map.158.rows_ref = bf16[80,256]{1,0:T(8,128)(2,1)} custom-call(bf16[256,2048]{1,0:T(8,128)(2,1)} %bitcast.16, bf16[64,2048]{1,0:T(8,128)(2,1)} %bitcast.17, bf16[2,2048,256]{2,1,0:T(8,128)(2,1)} %in_ref.1, bf16[64,2048]{1,0:T(8,128)(2,1)} %bitcast.18, bf16[256,2048]{1,0:T(8,128)(2,1)} %out_ref.1, bf16[4,2048]{1,0:T(4,128)(2,1)} %bitcast.20, ...), custom_call_target="tpu_custom_call" | custom-call | flops 2000000000 | bytes 8000000 | tf_op jit(solution)/shard_map/pallas_call | solution.py:527
  68.9 1.4 %shard_map.159 = (bf16[64,256]{1,0:T(8,128)(2,1)}, bf16[4,4,256]{2,1,0:T(4,128)(2,1)}) custom-call(bf16[80,256]{1,0:T(8,128)(2,1)} %shard_map.158.rows_ref, s32[1,4]{1,0:T(1,128)} %bitcast.15), custom_call_target="tpu_custom_call" | custom-call | tf_op jit(solution)/shard_map/pallas_call | solution.py:570
